TPU v7x, 256 devices: a whole 4x4x8 slice. The times are simulated.
256 devices in a mesh: grp: 8 (over z), tile: 32 (over x, y, core).
Axes of the slice: x: 4, y: 4, z: 8, core: 2. Of those that a mesh axis runs over, the one named last changes fastest.
Arguments:
- speed: float32 [128, 2, 32, 128], P('tile'), may hold values from 0.15 to 0.4
- density: float32 [128, 2, 32, 128], P('tile'), may hold values from 1 to 3
- fwd_state: bfloat16 [256, 4, 32, 32, 128], P(('grp', 'tile')), may hold values from -6 to 6
- adj_state: bfloat16 [256, 4, 32, 32, 128], P(('grp', 'tile')), may hold values from -6 to 6
- aperture: int32 [256, 16], P(('grp', 'tile')), may hold values from 0 to 127, as said below
- src_pos: int32 [256, 3], P(('grp', 'tile')), may hold values from 0 to 127, as said below
- wavelet: float32 [256, 4], P(('grp', 'tile')), may hold values from -15 to 15
- rec_pos: int32 [256, 32, 2], P(('grp', 'tile')), may hold values from 0 to 127, as said below
- residual: float32 [256, 4, 32], P(('grp', 'tile')), may hold values from -6 to 6
Outputs:
- grad_speed: float32 [128, 2, 32, 128], P('tile')
- grad_density: float32 [128, 2, 32, 128], P('tile')
Inputs may be any that keep to these rules, and one draw needn't show every extreme that they name: `aperture`: row s is (c + j) * 4 + e for j = 0 .. 15, with one c in 0 .. 16 and one e in 0 .. 3 for each shot, so a shot takes exactly one tile from each of 16 owners. `src_pos`: columns are x in 0 .. 31, y in 0 .. 31, z in 0 .. 127. `rec_pos`: columns are y in 0 .. 31 and z in 0 .. 127.
All inputs are finite; a program needn't handle non-finite values.
Results may differ from a plain program's by a relative error of at most 0.0003.
Values sent between devices are 32-bit elements; how exact they have to be, the bound alone decides.
A program may use at most 64 MiB of HBM per device.

v0:
```python
import math

import jax
import jax.numpy as jnp
from jax import lax
from jax.sharding import PartitionSpec as P

COEF = (1225.0 / 1024.0, -245.0 / 3072.0, 49.0 / 5120.0, -5.0 / 7168.0)


def padded_along(values, which_dim):
    widths = [(0, 0), (0, 0), (0, 0)]
    widths[which_dim] = (4, 4)
    return jnp.pad(values, widths)


def forward_diff(values, which_dim):
    length = values.shape[which_dim]
    padded = padded_along(values, which_dim)
    total = jnp.zeros_like(values)
    for order in range(1, 5):
        upper = lax.slice_in_dim(padded, 4 + order, 4 + order + length, axis=which_dim)
        lower = lax.slice_in_dim(padded, 5 - order, 5 - order + length, axis=which_dim)
        total = total + COEF[order - 1] * (upper - lower)
    return total


def backward_diff(values, which_dim):
    length = values.shape[which_dim]
    padded = padded_along(values, which_dim)
    total = jnp.zeros_like(values)
    for order in range(1, 5):
        upper = lax.slice_in_dim(padded, 3 + order, 3 + order + length, axis=which_dim)
        lower = lax.slice_in_dim(padded, 4 - order, 4 - order + length, axis=which_dim)
        total = total + COEF[order - 1] * (upper - lower)
    return total


def advance(pressure, velocity, bulk, buoyancy, source):
    moved = tuple(
        (
            velocity[which_dim] + buoyancy * forward_diff(pressure, which_dim)
            for which_dim in range(3)
        )
    )
    divergence = (
        backward_diff(moved[0], 0) + backward_diff(moved[1], 1) + backward_diff(moved[2], 2)
    )
    return (pressure + bulk * divergence + source, moved)


def evolve(speed_ap, density_ap, fwd_state, adj_state, src_pos, wavelet, rec_pos, residual):
    bulk = density_ap * speed_ap * speed_ap
    buoyancy = 1.0 / density_ap
    xs_cells = jnp.arange(speed_ap.shape[0], dtype=jnp.int32)
    ys_cells = jnp.arange(speed_ap.shape[1], dtype=jnp.int32)
    zs_cells = jnp.arange(speed_ap.shape[2], dtype=jnp.int32)
    src_mask = (
        (xs_cells == src_pos[0])[:, None, None]
        & (ys_cells == src_pos[1])[None, :, None]
        & (zs_cells == src_pos[2])[None, None, :]
    ).astype(jnp.float32)
    rec_mask = (
        (ys_cells[None, :, None] == rec_pos[:, 0][:, None, None])
        & (zs_cells[None, None, :] == rec_pos[:, 1][:, None, None])
    ).astype(jnp.float32)
    state = fwd_state.astype(jnp.float32)
    pressure = state[0]
    velocity = (state[1], state[2], state[3])
    changes = []
    steps_count = wavelet.shape[0]
    for step_index in range(steps_count):
        new_pressure, new_velocity = advance(
            pressure, velocity, bulk, buoyancy, wavelet[step_index] * src_mask
        )
        changes.append(
            (new_pressure - pressure, tuple((new_velocity[d] - velocity[d] for d in range(3))))
        )
        pressure, velocity = (new_pressure, new_velocity)
    adjoint = adj_state.astype(jnp.float32)
    adj_pressure = adjoint[0]
    adj_velocity = (adjoint[1], adjoint[2], adjoint[3])
    bulk_image = jnp.zeros_like(bulk)
    buoy_image = jnp.zeros_like(bulk)
    for step_index in reversed(range(steps_count)):
        adj_pressure, adj_velocity = advance(
            adj_pressure,
            adj_velocity,
            bulk,
            buoyancy,
            residual[step_index][:, None, None] * rec_mask,
        )
        bulk_image = bulk_image + changes[step_index][0] * adj_pressure
        dvel = changes[step_index][1]
        buoy_image = (
            buoy_image
            + dvel[0] * adj_velocity[0]
            + dvel[1] * adj_velocity[1]
            + dvel[2] * adj_velocity[2]
        )
    return (bulk_image, buoy_image)


def per_device(speed, density, fwd_state, adj_state, aperture, src_pos, wavelet, rec_pos, residual):
    owners = lax.axis_size("tile")
    myself = lax.axis_index("tile")
    held = speed.shape[0]
    tile_x, tile_y, depth = (speed.shape[1], speed.shape[2], speed.shape[3])
    stripes = aperture.shape[1]
    mine = aperture[0]
    lists = lax.all_gather(aperture, "tile", axis=0, tiled=True)
    owner_ids = jnp.arange(owners, dtype=jnp.int32)
    held_ids = jnp.arange(held, dtype=jnp.int32)
    matches = (lists // held == myself)[:, :, None] & (
        (lists % held)[:, :, None] == held_ids[None, None, :]
    )
    picked = jnp.sum(matches.astype(jnp.float32), axis=1)
    placed = (mine[:, None] // held == owner_ids[None, :]).astype(jnp.float32)
    highest = lax.Precision.HIGHEST
    pieces = (
        lax.all_gather(speed, "tile", axis=0, tiled=True),
        lax.all_gather(density, "tile", axis=0, tiled=True),
    )
    rows = pieces[0].shape[0]
    select = (mine[:, None] == jnp.arange(rows, dtype=jnp.int32)[None, :]).astype(jnp.float32)
    ap_speed = jnp.einsum("jt,txyz->jxyz", select, pieces[0], precision=highest)
    ap_density = jnp.einsum("jt,txyz->jxyz", select, pieces[1], precision=highest)
    speed_ap = ap_speed.reshape(stripes * tile_x, tile_y, depth)
    density_ap = ap_density.reshape(stripes * tile_x, tile_y, depth)
    bulk_image, buoy_image = evolve(
        speed_ap,
        density_ap,
        fwd_state[0],
        adj_state[0],
        src_pos[0],
        wavelet[0],
        rec_pos[0],
        residual[0],
    )
    bulk_parts = bulk_image.reshape(stripes, tile_x, tile_y, depth)
    buoy_parts = buoy_image.reshape(stripes, tile_x, tile_y, depth)
    back_bulk = jnp.einsum("jo,jxyz->oxyz", placed, bulk_parts, precision=highest)
    back_buoy = jnp.einsum("jo,jxyz->oxyz", placed, buoy_parts, precision=highest)
    came_bulk, came_buoy = (
        lax.all_to_all(back_bulk, "tile", split_axis=0, concat_axis=0, tiled=True),
        lax.all_to_all(back_buoy, "tile", split_axis=0, concat_axis=0, tiled=True),
    )
    own_bulk = jnp.einsum("rt,rxyz->txyz", picked, came_bulk, precision=highest)
    own_buoy = jnp.einsum("rt,rxyz->txyz", picked, came_buoy, precision=highest)
    bulk_sum, buoy_sum = lax.psum((own_bulk, own_buoy), "grp")
    scale = 1.0 / math.sqrt(lax.axis_size("grp") * owners)
    grad_speed = scale * (bulk_sum * (2.0 * density * speed))
    grad_density = scale * (bulk_sum * (speed * speed) - buoy_sum / (density * density))
    return (grad_speed, grad_density)


def solution(mesh):
    return jax.shard_map(
        per_device,
        mesh=mesh,
        in_specs=(
            P("tile", None, None, None),
            P("tile", None, None, None),
            P(("grp", "tile"), None, None, None, None),
            P(("grp", "tile"), None, None, None, None),
            P(("grp", "tile"), None),
            P(("grp", "tile"), None),
            P(("grp", "tile"), None),
            P(("grp", "tile"), None, None),
            P(("grp", "tile"), None, None),
        ),
        out_specs=(P("tile", None, None, None), P("tile", None, None, None)),
        check_vma=False,
    )
```

profile of v0, /device:TPU:2, one launch (start us, length us, event | category | flops | bytes accessed | tf_op | source)
XLA Modules:
  0.0 306.5 jit_solution(4750725316067010165)
XLA Ops:
  7.2 0.0 copy-start.8
  7.2 0.0 copy-start.6
  7.2 0.0 copy-start.7
  7.2 0.0 copy-start.10
  7.2 0.0 copy-start.9
  7.2 0.0 all-gather.4.cloned.1.call-start
  7.3 0.7 all-gather.4.cloned.1.call-update
  8.0 0.0 all-gather.6.cloned.1.call-start
  8.0 0.7 all-gather.6.cloned.1.call-update
  8.7 1.5 convert_element_type.67
  10.2 1.5 convert_element_type.68
  11.7 0.0 copy-done.8
  11.7 0.0 copy-start
  11.7 0.7 fusion.658
  12.5 0.6 iota_compare_fusion.5
  13.1 1.3 iota_compare_fusion.6
  14.4 0.0 copy-done.6
  14.4 0.7 fusion.657
  15.1 0.0 copy-done.7
  15.1 0.0 copy-done.10
  15.1 0.1 iota_compare_fusion.1
  15.2 0.1 iota_compare_fusion.2
  15.3 0.1 broadcast_and_fusion
  15.4 0.0 copy-done
  15.4 0.9 slice_bitcast_fusion.3
  16.2 48.1 %all-gather.4.cloned.1.call-done = f32[128,2,32,128]{3,2,1,0:T(8,128)} async-done(((f32[4,2,32,128]{3,2,1,0:T(8,128)}), f32[128,2,32,128]{3,2,1,0:T(8,128)}) %all-gather.4.cloned.1.call-update) | async-done | bytes 4194320 | tf_op jit(solution)/shard_map/all_gather | solution.py:122
  64.4 5.8 %fusion.2 = f32[16,2,32,128]{3,0,2,1:T(8,128)S(1)} fusion(f32[128,2,32,128]{3,2,1,0:T(8,128)} %all-gather.4.cloned.1.call-done, s32[16]{0:T(128)S(1)} %bitcast.173), kind=kOutput, calls=%fused_computation.2 | convolution fusion | flops 201328640 | bytes 4718656 | tf_op jit(solution)/shard_map/jt,txyz->jxyz/dot_general | solution.py:127
  70.2 0.2 copy.73
  70.4 47.1 %all-gather.6.cloned.1.call-done = f32[128,2,32,128]{3,2,1,0:T(8,128)} async-done(((f32[4,2,32,128]{3,2,1,0:T(8,128)}), f32[128,2,32,128]{3,2,1,0:T(8,128)}) %all-gather.6.cloned.1.call-update) | async-done | bytes 4194320 | tf_op jit(solution)/shard_map/all_gather | solution.py:121
  117.5 6.0 %fusion = f32[16,2,32,128]{3,0,2,1:T(8,128)S(1)} fusion(f32[128,2,32,128]{3,2,1,0:T(8,128)} %all-gather.6.cloned.1.call-done, s32[16]{0:T(128)S(1)} %bitcast.174), kind=kOutput, calls=%fused_computation | convolution fusion | flops 201328640 | bytes 4718656 | tf_op jit(solution)/shard_map/jt,txyz->jxyz/dot_general | solution.py:126
  123.5 0.2 copy.75
  123.7 3.0 fusion.540
  126.7 2.3 fusion.30
  129.0 1.6 fusion.247
  130.6 2.8 fusion.313
  133.4 1.6 fusion.300
  135.0 2.2 fusion.83
  137.2 2.8 fusion.337
  140.0 1.6 fusion.353
  141.6 2.2 fusion.136
  143.8 4.9 %multiply_add_fusion = (f32[32,32,128]{2,1,0:T(8,128)}, f32[32,32,128]{2,1,0:T(8,128)}, f32[32,32,128]{2,1,0:T(8,128)}, f32[32,32,128]{2,1,0:T(8,128)}, f32[32,3...) fusion(f32[32,32,128]{2,1,0:T(8,128)S(1)} %get-tuple-element.49, ...), kind=kLoop, calls=%fused_computation.988 | loop fusion | flops 14942208 | bytes 16252928 | tf_op jit(solution)/shard_map/add | solution.py:96
  148.7 14.3 %fusion.194 = f32[32,32,128]{2,1,0:T(8,128)S(1)} fusion(f32[32,32,128]{2,1,0:T(8,128)S(1)} %fusion.247, f32[32,32,128]{2,1,0:T(8,128)S(1)} %fusion.136, f32[32,32,128]{2,1,0:T(8,128)S(1)} %get-tuple-element.22, f32[32,32,128]{2,1,0:T(8,128)} %get-tuple-element.20, f32[32,32,128]{2,1,0:T(8,128)} %get-tuple-element.19, f32[32,32,128]{2,1,0:T(8,128)S(1)} %fusion.353, ...), kind=kLoop, calls=%fused_computation.539 | loop fusion | flops 11927552 | bytes 7870724 | tf_op jit(solution)/shard_map/add | solution.py:93
  163.1 0.9 fusion.632
  164.0 1.6 copy.77
  165.6 5.9 %all-to-all-start = ((f32[32,2,32,128]{3,2,1,0:T(8,128)}), f32[32,2,32,128]{3,2,1,0:T(8,128)S(1)}, u32[]{:S(2)}, u32[]{:S(2)}) async-start(f32[32,2,32,128]{3,2,1,0:T(8,128)} %copy.77), calls=%async_computation | async-start | bytes 2097152 | tf_op jit(solution)/shard_map/all_to_all | solution.py:145
  171.4 0.0 copy-done.2
  171.4 0.0 copy-start.4
  171.5 0.0 copy-start.5
  171.5 0.9 fusion.630
  172.4 1.6 copy.84
  173.9 11.9 %all-to-all-done = f32[32,2,32,128]{3,2,1,0:T(8,128)S(1)} async-done(((f32[32,2,32,128]{3,2,1,0:T(8,128)}), f32[32,2,32,128]{3,2,1,0:T(8,128)S(1)}, u32[]{:S(2)}, u32[]{:S(2)}) %all-to-all-start) | async-done | bytes 1048608 | tf_op jit(solution)/shard_map/all_to_all | solution.py:145
  185.9 6.4 %all-to-all-start.1 = ((f32[32,2,32,128]{3,2,1,0:T(8,128)}), f32[32,2,32,128]{3,2,1,0:T(8,128)S(1)}, u32[]{:S(2)}, u32[]{:S(2)}) async-start(f32[32,2,32,128]{3,2,1,0:T(8,128)} %copy.84), calls=%async_computation.1 | async-start | bytes 2097152 | tf_op jit(solution)/shard_map/all_to_all | solution.py:146
  192.3 0.0 all-reduce.51.cloned.1.call-start
  192.4 29.0 %all-gather = s32[32,1,16]{2,1,0:T(1,128)S(1)} all-gather(s32[1,1,16]{2,1,0:T(1,128)S(1)} %bitcast.175), channel_id=1, replica_groups=mesh['grp'=8,'tile'=32] {'tile'}, dimensions={0}, use_global_device_ids=true | all-gather | bytes 2112 | tf_op jit(solution)/shard_map/all_gather | solution.py:111
  221.4 0.1 copy.71
  221.5 1.8 fusion.6
  223.3 0.0 all-to-all-done.1
  223.3 1.8 fusion.4
  225.1 0.0 all-reduce.51.cloned.1.call-update
  225.2 72.3 %all-reduce.51.cloned.1.call-done = (f32[4,2,32,128]{3,0,2,1:T(4,128)}, f32[4,2,32,128]{3,0,2,1:T(4,128)}) async-done(((f32[4,2,32,128]{3,0,2,1:T(4,128)}, f32[4,2,32,128]{3,0,2,1:T(4,128)}), (f32[4,2,32,128]{3,0,2,1:T(4,128)}, f32[4,2,32,128]{3,0,2,1:T(4,128)})) %all-reduce.51.cloned.1.call-update) | async-done | bytes 262160 | tf_op jit(solution)/shard_map/psum | solution.py:150
  297.5 0.0 copy-done.5
  297.5 1.2 subtract_multiply_fusion
  298.7 0.7 copy.88
  299.3 0.7 copy.89
  (13 shorter events, 0.1 us)
Async XLA Ops:
  7.2 4.6 %copy-start.8 = (s32[1,3]{1,0:T(1,128)S(1)}, s32[1,3]{1,0:T(1,128)}, u32[]{:S(2)}) copy-start(s32[1,3]{1,0:T(1,128)} %param.14) | copy-start | bytes 40
  7.2 7.2 %copy-start.6 = (f32[1,4]{1,0:T(1,128)S(1)}, f32[1,4]{1,0:T(1,128)}, u32[]{:S(2)}) copy-start(f32[1,4]{1,0:T(1,128)} %param.15) | copy-start | bytes 52
  7.2 7.9 %copy-start.7 = (s32[1,16]{1,0:T(1,128)S(1)}, s32[1,16]{1,0:T(1,128)}, u32[]{:S(2)}) copy-start(s32[1,16]{1,0:T(1,128)} %param.13) | copy-start | bytes 196
  7.2 7.9 %copy-start.10 = (s32[1,32,2]{1,2,0:T(2,128)S(1)}, s32[1,32,2]{1,2,0:T(2,128)}, u32[]{:S(2)}) copy-start(s32[1,32,2]{1,2,0:T(2,128)} %param.16) | copy-start | bytes 772
  7.2 7.9 %copy-start.9 = (f32[1,4,32]{2,1,0:T(4,128)S(1)}, f32[1,4,32]{2,1,0:T(4,128)}, u32[]{:S(2)}) copy-start(f32[1,4,32]{2,1,0:T(4,128)} %param.17) | copy-start | bytes 1540
  7.2 57.1 %all-gather.4.cloned.1.call-start = ((), (), s32[]{:S(2)}) async-start(), calls=%async_computation.2 | async-start | bytes 4325376 | tf_op jit(solution)/shard_map/all_gather | solution.py:122
  8.0 109.5 %all-gather.6.cloned.1.call-start = ((), (), s32[]{:S(2)}) async-start(), calls=%async_computation.3 | async-start | bytes 4325376 | tf_op jit(solution)/shard_map/all_gather | solution.py:121
  11.7 3.6 %copy-start = (f32[1,4,32,32,128]{4,3,2,1,0:T(8,128)}, f32[1,4,32,32,128]{4,3,2,1,0:T(8,128)S(1)}, u32[]{:S(2)}) copy-start(f32[1,4,32,32,128]{4,3,2,1,0:T(8,128)S(1)} %convert_element_type.68) | copy-start | bytes 6291460
  117.5 6.2 %copy-start.1 = (f32[1,4,32,32,128]{4,3,2,1,0:T(8,128)S(1)}, f32[1,4,32,32,128]{4,3,2,1,0:T(8,128)}, u32[]{:S(2)}) copy-start(f32[1,4,32,32,128]{4,3,2,1,0:T(8,128)} %copy-done) | copy-start | bytes 6291460
  117.5 6.2 %copy-start.3 = (f32[32,32,128]{2,1,0:T(8,128)S(1)}, f32[32,32,128]{2,1,0:T(8,128)}, u32[]{:S(2)}) copy-start(f32[32,32,128]{2,1,0:T(8,128)} %get-tuple-element.66) | copy-start | bytes 1572868
  163.1 8.4 %copy-start.2 = (f32[32,32,128]{2,1,0:T(8,128)S(1)}, f32[32,32,128]{2,1,0:T(8,128)}, u32[]{:S(2)}) copy-start(f32[32,32,128]{2,1,0:T(8,128)} %get-tuple-element.14) | copy-start | bytes 1572868
  165.6 20.3 %all-to-all-start = ((f32[32,2,32,128]{3,2,1,0:T(8,128)}), f32[32,2,32,128]{3,2,1,0:T(8,128)S(1)}, u32[]{:S(2)}, u32[]{:S(2)}) async-start(f32[32,2,32,128]{3,2,1,0:T(8,128)} %copy.77), calls=%async_computation | async-start | bytes 2097152 | tf_op jit(solution)/shard_map/all_to_all | solution.py:145
  171.4 126.0 %copy-start.4 = (f32[4,2,32,128]{3,2,1,0:T(8,128)S(1)}, f32[4,2,32,128]{3,2,1,0:T(8,128)}, u32[]{:S(2)}) copy-start(f32[4,2,32,128]{3,2,1,0:T(8,128)} %param.10) | copy-start | bytes 393220
  171.5 126.0 %copy-start.5 = (f32[4,2,32,128]{3,2,1,0:T(8,128)S(1)}, f32[4,2,32,128]{3,2,1,0:T(8,128)}, u32[]{:S(2)}) copy-start(f32[4,2,32,128]{3,2,1,0:T(8,128)} %param.9) | copy-start | bytes 393220
  185.9 37.5 %all-to-all-start.1 = ((f32[32,2,32,128]{3,2,1,0:T(8,128)}), f32[32,2,32,128]{3,2,1,0:T(8,128)S(1)}, u32[]{:S(2)}, u32[]{:S(2)}) async-start(f32[32,2,32,128]{3,2,1,0:T(8,128)} %copy.84), calls=%async_computation.1 | async-start | bytes 2097152 | tf_op jit(solution)/shard_map/all_to_all | solution.py:146
  192.3 105.2 %all-reduce.51.cloned.1.call-start = ((), (), s32[]{:S(2)}) async-start(), calls=%async_computation.4 | async-start | bytes 524288 | tf_op jit(solution)/shard_map/psum | solution.py:150
Sparse Core Ops, SparseCore 0:
  10.6 53.7 all-gather.3
  66.9 50.5 all-gather.5
  225.3 72.1 all-reduce.50
where the time goes:
time: 307 us
  waiting for transfers between devices  181 us (59%)
  other arithmetic  45.7 us (15%)
  blocking collectives  29 us (9%)
  matrix products  17.3 us (6%)
  between operations  14.1 us (5%)
  starting transfers between devices  12.4 us (4%)
  local copies, waits for them, and re-layouts  7.24 us (2%)
    psum x1, waiting for transfers between devices, per_device(): bulk_sum, buoy_sum = lax.psum((own_bulk, own_buoy), 'grp')  72.3 us
    all_gather x1, waiting for transfers between devices, per_device(): lax.all_gather(density, 'tile', axis=0, tiled=True)  48.1 us
    all_gather x1, waiting for transfers between devices, per_device(): lax.all_gather(speed, 'tile', axis=0, tiled=True)  47.1 us
    all_gather x1, blocking collectives, per_device(): lists = lax.all_gather(aperture, 'tile', axis=0, tiled=True)  29 us
    add x1, other arithmetic, evolve(): bulk_image = bulk_image + changes[step_index][0] * adj_pressure  14.3 us
    all_to_all x1, waiting for transfers between devices, per_device(): lax.all_to_all(back_bulk, 'tile', split_axis=0, concat_axis=0, tiled=True)  11.9 us
    add x6, other arithmetic, advance(): return (pressure + bulk * divergence + source, moved)  11.4 us
    add x3, other arithmetic, advance(): velocity[which_dim] + buoyancy * forward_diff(pressure, which_dim)  8.67 us
  transfers between devices with their start and end apart: 5, of which 4 were waited for; matrix products, arithmetic and copies ran while one was open for 6% of the time, Pallas kernels for 0%

commit v1 on v0

v1 whole, which is shorter than its diff:
```python
import math

import jax
import jax.numpy as jnp
import numpy as np
from jax import lax
from jax.experimental import pallas as pl
from jax.experimental.pallas import tpu as pltpu
from jax.sharding import PartitionSpec as P

COEF = (1225.0 / 1024.0, -245.0 / 3072.0, 49.0 / 5120.0, -5.0 / 7168.0)
SCALE = COEF[0] / (165.0 / 128.0)
TAPS = tuple(np.asarray(np.array(COEF) / SCALE, dtype=jnp.bfloat16).astype(np.float64).tolist())
STEPS = 4
NX, NY, NZ = 32, 32, 128
GROUP = 8 * NY
GROUPS = NX // 8
PAD = 4 * NY
CELLS = NX * NY


def difference_matrix(size, blocks):
    plus = np.zeros((size, size))
    for k in range(1, 5):
        plus += TAPS[k - 1] * (np.eye(size, k=k) - np.eye(size, k=1 - k))
    return np.kron(np.eye(blocks), plus)


def split(values):
    high = values.astype(jnp.bfloat16)
    low = (values - high.astype(jnp.float32)).astype(jnp.bfloat16)
    return jnp.concatenate([high, low], axis=1)


def along_y(matrix, parts):
    both = jnp.dot(matrix, parts, preferred_element_type=jnp.float32)
    return both[:, :NZ] + both[:, NZ:]


def along_z(parts, matrix):
    return jnp.dot(parts, matrix, preferred_element_type=jnp.float32)


def along_x(ref, base, backward):
    first = base + PAD - (NY if backward else 0)

    def plane(k):
        return ref[pl.ds(first + k * NY, GROUP), :]

    total = None
    for k in range(1, 5):
        term = TAPS[k - 1] * (plane(k) - plane(1 - k))
        total = term if total is None else total + term
    return total


def evolve_kernel(
    ap, src, wave, recs, resid, yplus_ref, yminus_ref, zplus_ref, zminus_ref,
    model, fwd, adj, image,
    pres, vel0, vel1, vel2, bulk, buoy, dpres, dvel, bulk_im, buoy_im,
):
    corner = ap[0, 0] // 4
    for j in range(16):
        slot = lax.rem(corner + j, 16)
        rows = pl.ds(j * 2 * NY, 2 * NY)
        bulk[rows, :] = SCALE * model[slot, 0]
        buoy[rows, :] = SCALE * model[slot, 1]
    edge = jnp.zeros((PAD, NZ), jnp.float32)
    for ref in (pres, vel0):
        ref[0:PAD, :] = edge
        ref[PAD + CELLS :, :] = edge
    lanes = lax.broadcasted_iota(jnp.int32, (1, NZ), 1)

    def load(state):
        for g in range(GROUPS):
            rows = pl.ds(g * GROUP, GROUP)
            padded = pl.ds(PAD + g * GROUP, GROUP)
            pres[padded, :] = state[0, 0, rows, :].astype(jnp.float32)
            vel0[padded, :] = state[0, 1, rows, :].astype(jnp.float32)
            vel1[rows, :] = state[0, 2, rows, :].astype(jnp.float32)
            vel2[rows, :] = state[0, 3, rows, :].astype(jnp.float32)

    def step(n, adjoint, first):
        for g in range(GROUPS):
            base = g * GROUP
            rows = pl.ds(base, GROUP)
            padded = pl.ds(PAD + base, GROUP)
            light = buoy[rows, :]
            parts = split(pres[padded, :])
            changes = (
                light * along_x(pres, base, False),
                light * along_y(yplus_ref[...], parts),
                light * along_z(parts, zplus_ref[...]),
            )
            total = None
            for d, (ref, where) in enumerate(((vel0, padded), (vel1, rows), (vel2, rows))):
                moved = ref[where, :] + changes[d]
                ref[where, :] = moved
                if adjoint:
                    term = dvel[n, d, rows, :] * moved
                    total = term if total is None else total + term
                else:
                    dvel[n, d, rows, :] = changes[d]
            if adjoint:
                buoy_im[rows, :] = total if first else buoy_im[rows, :] + total
        for g in range(GROUPS):
            base = g * GROUP
            rows = pl.ds(base, GROUP)
            padded = pl.ds(PAD + base, GROUP)
            divergence = (
                along_x(vel0, base, True)
                + along_y(yminus_ref[...], split(vel1[rows, :]))
                + along_z(split(vel2[rows, :]), zminus_ref[...])
            )
            change = bulk[rows, :] * divergence
            moved = pres[padded, :] + change
            pres[padded, :] = moved
            if adjoint:
                term = dpres[n, rows, :] * moved
                bulk_im[rows, :] = term if first else bulk_im[rows, :] + term
            else:
                dpres[n, rows, :] = change
        if adjoint:
            for j in range(NX):
                row = j * NY + recs[0, 2 * j]
                added = jnp.where(lanes == recs[0, 2 * j + 1], resid[0, n * NX + j], 0.0)
                at = pl.ds(row, 1)
                pres[pl.ds(PAD + row, 1), :] += added
                bulk_im[at, :] += dpres[n, at, :] * added
        else:
            row = src[0, 0] * NY + src[0, 1]
            added = jnp.where(lanes == src[0, 2], wave[0, n], 0.0)
            pres[pl.ds(PAD + row, 1), :] += added
            dpres[n, pl.ds(row, 1), :] += added

    load(fwd)

    def forward(n, carry):
        step(n, False, False)
        return carry

    lax.fori_loop(0, STEPS, forward, 0)
    load(adj)
    bulk_im[...] = jnp.zeros_like(bulk_im)
    buoy_im[...] = jnp.zeros_like(buoy_im)

    def backward(n, carry):
        step(STEPS - 1 - n, True, False)
        return carry

    lax.fori_loop(0, STEPS, backward, 0)
    for j in range(16):
        slot = lax.rem(corner + j, 16)
        rows = pl.ds(j * 2 * NY, 2 * NY)
        image[slot, 0] = bulk_im[rows, :]
        image[slot, 1] = buoy_im[rows, :]


def evolve(model, fwd_state, adj_state, aperture, src_pos, wavelet, rec_pos, residual):
    yplus = difference_matrix(NY, 8)
    zplus = difference_matrix(NZ, 1)
    matrices = [
        jnp.asarray(m, jnp.bfloat16)
        for m in (yplus, -yplus.T, np.concatenate([zplus.T, zplus.T]), np.concatenate([-zplus, -zplus]))
    ]
    smem = pl.BlockSpec(memory_space=pltpu.SMEM)
    vmem = pl.BlockSpec(memory_space=pltpu.VMEM)
    field = pltpu.VMEM((CELLS, NZ), jnp.float32)
    wide = pltpu.VMEM((CELLS + 2 * PAD, NZ), jnp.float32)
    return pl.pallas_call(
        evolve_kernel,
        out_shape=jax.ShapeDtypeStruct((16, 2, 2 * NY, NZ), jnp.float32),
        in_specs=[smem] * 5 + [vmem] * 7,
        out_specs=vmem,
        scratch_shapes=[
            wide, wide, field, field, field, field,
            pltpu.VMEM((STEPS, CELLS, NZ), jnp.float32),
            pltpu.VMEM((STEPS, 3, CELLS, NZ), jnp.float32),
            field, field,
        ],
        compiler_params=pltpu.CompilerParams(vmem_limit_bytes=40 * 1024 * 1024),
        cost_estimate=pl.CostEstimate(flops=10**9, bytes_accessed=5 * 2**20, transcendentals=0),
    )(
        aperture, src_pos, wavelet, rec_pos.reshape(1, -1), residual.reshape(1, -1), *matrices, model,
        fwd_state.reshape(1, 4, CELLS, NZ), adj_state.reshape(1, 4, CELLS, NZ),
    )

MESH = pl.DeviceIdType.MESH
FIELDS = 2
TILES = 4


def place():
    tile = lax.axis_index("tile")
    return tile // 8, lax.rem(tile // 2, 4), lax.rem(tile, 2)


def tile_at(x, y, core):
    return lax.rem(x + 4, 4) * 8 + lax.rem(y + 4, 4) * 2 + lax.rem(core, 2)


def remote(source, target, send, receive, device):
    return pltpu.make_async_remote_copy(
        src_ref=source, dst_ref=target, send_sem=send, recv_sem=receive,
        device_id=device, device_id_type=MESH,
    )


def greet(devices):
    barrier = pltpu.get_barrier_semaphore()
    for device in devices:
        pl.semaphore_signal(barrier, inc=1, device_id=device, device_id_type=MESH)
    return lambda: pl.semaphore_wait(barrier, len(devices))


def matches(code, residue):
    corner, level = code >> 2, code & 3
    upper = corner > residue
    return [
        [jnp.logical_and(level == t, upper if high else jnp.logical_not(upper)) for t in range(TILES)]
        for high in range(2)
    ]


def gather_kernel(
    ap, speed, density, model, codes, row, staged, x_send, x_recv, c_send, c_recv, y_send, y_recv
):
    x, y, core = place()
    right, left = {"tile": tile_at(x + 1, y, core)}, {"tile": tile_at(x - 1, y, core)}
    ahead = [{"tile": tile_at(x, y + j // 2, core + j % 2)} for j in range(8)]
    back = [{"tile": tile_at(x, y - j // 2, core + j % 2)} for j in range(8)]
    ready = greet([right, left] + ahead[1:])
    codes[0] = jnp.zeros((8, NZ), jnp.int32) + ap[0, 0]
    for t in range(TILES):
        dense, fast = density[t], speed[t]
        row[0, x, t] = dense * fast * fast
        row[1, x, t] = 1.0 / dense
    ready()
    xl, xr, x2 = lax.rem(x + 3, 4), lax.rem(x + 1, 4), lax.rem(x + 2, 4)
    pending = []

    def start(copy):
        copy.start()
        pending.append(copy)

    for j in range(1, 8):
        start(remote(codes.at[0], codes.at[j], c_send.at[j], c_recv.at[j], ahead[j]))
    for f in range(FIELDS):
        for side, device in ((0, right), (1, left)):
            start(remote(row.at[f, x], row.at[f, x], x_send.at[0, side, f], x_recv.at[0, side, f], device))

    def forward(f):
        for side, device, origin in ((0, right, xl), (1, left, xr)):
            part = row.at[f, origin]
            remote(part, part, x_send.at[0, side, f], x_recv.at[0, side, f], device).wait_recv()
            half = row.at[f, origin, pl.ds(2 * side, 2)]
            start(remote(half, half, x_send.at[1, side, f], x_recv.at[1, side, f], device))

    def passed_on(f):
        for side, device in ((0, right), (1, left)):
            half = row.at[f, x2, pl.ds(2 * side, 2)]
            remote(half, half, x_send.at[1, side, f], x_recv.at[1, side, f], device).wait_recv()

    def select(code, parity, f):
        found = matches(code, parity * 8 + y * 2 + core)
        chosen = jnp.zeros((8, 8, NZ), jnp.float32)
        for high in range(2):
            for t in range(TILES):
                chosen = jnp.where(found[high][t][None], row[f, parity + 2 * high, t], chosen)
        return chosen

    mine = y * 2 + core

    def serve(parity, own, f):
        for j in (2, 3, 6, 7, 4, 5, 1):
            if own == 0 and f == 0:
                remote(codes.at[0], codes.at[j], c_send.at[j], c_recv.at[j], ahead[j]).wait_recv()
            staged[own, f, j] = select(codes[j], parity, f)
            start(
                remote(
                    staged.at[own, f, j], model.at[parity, mine, f],
                    y_send.at[own, f, j], y_recv.at[own, f, j], back[j],
                )
            )
        model[parity, mine, f] = select(codes[0], parity, f)

    other, same = lax.rem(x + 1, 2), lax.rem(x, 2)
    forward(0)
    serve(other, 0, 0)
    forward(1)
    serve(other, 0, 1)
    passed_on(0)
    serve(same, 1, 0)
    passed_on(1)
    serve(same, 1, 1)
    for own, parity in ((0, other), (1, same)):
        for f in range(FIELDS):
            for j in range(1, 8):
                origin = lax.rem(y + j // 2, 4) * 2 + lax.rem(core + j % 2, 2)
                remote(
                    staged.at[own, f, j], model.at[parity, origin, f],
                    y_send.at[own, f, j], y_recv.at[own, f, j], back[j],
                ).wait_recv()
    for copy in pending:
        copy.wait_send()


def gather(aperture, speed, density):
    vmem = pl.BlockSpec(memory_space=pltpu.VMEM)
    dma = pltpu.SemaphoreType.DMA
    return pl.pallas_call(
        gather_kernel,
        out_shape=(
            jax.ShapeDtypeStruct((2, 8, FIELDS, 8, 8, NZ), jnp.float32),
            jax.ShapeDtypeStruct((8, 8, NZ), jnp.int32),
        ),
        in_specs=[pl.BlockSpec(memory_space=pltpu.SMEM), vmem, vmem],
        out_specs=(vmem, vmem),
        scratch_shapes=[
            pltpu.VMEM((FIELDS, 4, TILES, 8, 8, NZ), jnp.float32),
            pltpu.VMEM((2, FIELDS, 8, 8, 8, NZ), jnp.float32),
            dma((2, 2, FIELDS)), dma((2, 2, FIELDS)), dma((8,)), dma((8,)),
            dma((2, FIELDS, 8)), dma((2, FIELDS, 8)),
        ],
        compiler_params=pltpu.CompilerParams(
            collective_id=0, has_side_effects=True, vmem_limit_bytes=16 * 1024 * 1024
        ),
        cost_estimate=pl.CostEstimate(flops=10**6, bytes_accessed=60 * 2**20, transcendentals=0),
    )(aperture, speed.reshape(TILES, 8, 8, NZ), density.reshape(TILES, 8, 8, NZ))


def scatter_kernel(
    codes, image, speed, density, grad_speed, grad_density,
    came, part, passed, summed, total, terms,
    y_send, y_recv, x_send, x_recv, z_send, z_recv, g_send, g_recv,
):
    z = lax.axis_index("grp")
    x, y, core = place()
    right, left = {"tile": tile_at(x + 1, y, core)}, {"tile": tile_at(x - 1, y, core)}
    ahead = [{"tile": tile_at(x, y + j // 2, core + j % 2)} for j in range(8)]
    column = [{"grp": lax.rem(z + d, 8)} for d in range(8)]
    greet([right, left] + ahead[1:] + column[1:])()
    xl, xr, x2 = lax.rem(x + 3, 4), lax.rem(x + 1, 4), lax.rem(x + 2, 4)
    mine = y * 2 + core
    pending = []

    def start(copy):
        copy.start()
        pending.append(copy)

    other, same = lax.rem(x + 1, 2), lax.rem(x, 2)
    chunks = [(own, parity, f) for own, parity in ((1, same), (0, other)) for f in range(FIELDS)]

    def image_copy(own, parity, f, j):
        target = lax.rem(y + j // 2, 4) * 2 + lax.rem(core + j % 2, 2)
        return remote(
            image.at[parity, target, f], came.at[own, f, j], y_send.at[own, f, j], y_recv.at[own, f, j], ahead[j]
        )

    for own, parity, f in chunks:
        for j in (2, 3, 6, 7, 4, 5, 1):
            start(image_copy(own, parity, f, j))

    def collect(own, parity, f):
        for j in range(1, 8):
            image_copy(own, parity, f, j).wait_recv()
        found = [matches(codes[j], parity * 8 + mine) for j in range(8)]
        for high in range(2):
            for t in range(TILES):
                held = None
                for j in range(8):
                    values = image[parity, mine, f] if j == 0 else came[own, f, j]
                    term = jnp.where(found[j][high][t][None], values, 0.0)
                    held = term if held is None else held + term
                part[f, parity + 2 * high, t] = held

    def hop(stage, side, f):
        device, target = ((right, xr), (left, xl))[side]
        if stage == 0:
            return remote(
                part.at[f, x2, pl.ds(2 * side, 2)], passed.at[side, f],
                x_send.at[0, side, f], x_recv.at[0, side, f], device,
            )
        return remote(
            part.at[f, target], summed.at[side, f], x_send.at[1, side, f], x_recv.at[1, side, f], device
        )

    def piece_copy(f, d):
        return remote(
            total.at[f, lax.rem(z + d, 8)], terms.at[f, d], z_send.at[f, d], z_recv.at[f, d], column[d]
        )

    for f in range(FIELDS):
        collect(1, same, f)
        for side in range(2):
            start(hop(0, side, f))
    for f in range(FIELDS):
        collect(0, other, f)
        for side in range(2):
            target = (xr, xl)[side]
            hop(0, side, f).wait_recv()
            for i in range(2):
                part[f, target, 2 * side + i] += passed[side, f, i]
            start(hop(1, side, f))
    for f in range(FIELDS):
        for side in range(2):
            hop(1, side, f).wait_recv()
        for t in range(TILES):
            whole = part[f, x, t] + summed[0, f, t] + summed[1, f, t]
            total[f, 2 * t] = whole[:4]
            total[f, 2 * t + 1] = whole[4:]
        for d in (1, 7, 2, 6, 3, 5, 4):
            start(piece_copy(f, d))
    sums = []
    for f in range(FIELDS):
        whole = total[f, z]
        for d in range(1, 8):
            piece_copy(f, d).wait_recv()
            whole = whole + terms[f, d]
        sums.append(whole)
    fast, dense = speed[z], density[z]
    factor = 1.0 / math.sqrt(256.0)
    grad_speed[z] = factor * (sums[0] * (2.0 * dense * fast))
    grad_density[z] = factor * (sums[0] * (fast * fast) - sums[1] / (dense * dense))

    def result_copy(i, d, piece):
        ref = (grad_speed, grad_density)[i]
        return remote(ref.at[piece], ref.at[piece], g_send.at[i, d], g_recv.at[i, d], column[d])

    for d in (1, 7, 2, 6, 3, 5, 4):
        for i in range(2):
            start(result_copy(i, d, z))
    for d in range(1, 8):
        for i in range(2):
            result_copy(i, d, lax.rem(z + 8 - d, 8)).wait_recv()
    for copy in pending:
        copy.wait_send()


def scatter(codes, image, speed, density):
    vmem = pl.BlockSpec(memory_space=pltpu.VMEM)
    dma = pltpu.SemaphoreType.DMA
    shape = jax.ShapeDtypeStruct((8, 4, 8, NZ), jnp.float32)
    return pl.pallas_call(
        scatter_kernel,
        out_shape=(shape, shape),
        in_specs=[vmem] * 4,
        out_specs=(vmem, vmem),
        scratch_shapes=[
            pltpu.VMEM((2, FIELDS, 8, 8, 8, NZ), jnp.float32),
            pltpu.VMEM((FIELDS, 4, TILES, 8, 8, NZ), jnp.float32),
            pltpu.VMEM((2, FIELDS, 2, 8, 8, NZ), jnp.float32),
            pltpu.VMEM((2, FIELDS, TILES, 8, 8, NZ), jnp.float32),
            pltpu.VMEM((FIELDS, 8, 4, 8, NZ), jnp.float32),
            pltpu.VMEM((FIELDS, 8, 4, 8, NZ), jnp.float32),
            dma((2, FIELDS, 8)), dma((2, FIELDS, 8)), dma((2, 2, FIELDS)), dma((2, 2, FIELDS)),
            dma((FIELDS, 8)), dma((FIELDS, 8)), dma((2, 8)), dma((2, 8)),
        ],
        compiler_params=pltpu.CompilerParams(
            collective_id=1, has_side_effects=True, vmem_limit_bytes=16 * 1024 * 1024
        ),
        cost_estimate=pl.CostEstimate(flops=10**6, bytes_accessed=60 * 2**20, transcendentals=0),
    )(codes, image, speed.reshape(8, 4, 8, NZ), density.reshape(8, 4, 8, NZ))


def per_device(speed, density, fwd_state, adj_state, aperture, src_pos, wavelet, rec_pos, residual):
    model, codes = gather(aperture, speed, density)
    image = evolve(
        model.reshape(16, FIELDS, 2 * NY, NZ), fwd_state, adj_state, aperture, src_pos, wavelet, rec_pos, residual
    )
    grads = scatter(codes, image.reshape(2, 8, FIELDS, 8, 8, NZ), speed, density)
    return tuple(grad.reshape(speed.shape) for grad in grads)


def solution(mesh):
    return jax.shard_map(
        per_device,
        mesh=mesh,
        in_specs=(
            P("tile", None, None, None),
            P("tile", None, None, None),
            P(("grp", "tile"), None, None, None, None),
            P(("grp", "tile"), None, None, None, None),
            P(("grp", "tile"), None),
            P(("grp", "tile"), None),
            P(("grp", "tile"), None),
            P(("grp", "tile"), None, None),
            P(("grp", "tile"), None, None),
        ),
        out_specs=(P("tile", None, None, None), P("tile", None, None, None)),
        check_vma=False,
    )
```

time: 307 us -> 89.7 us (0.29)
  waiting for transfers between devices: 181 us -> 0 us
  Pallas kernels: 0 us -> 77.6 us
  other arithmetic: 45.7 us -> 0 us
  blocking collectives: 29 us -> 0 us
  matrix products: 17.3 us -> 0 us
  between operations: 14.1 us -> 0.73 us
  starting transfers between devices: 12.4 us -> 0 us
    all_gather x2 -> x0, waiting for transfers between devices: 95.2 us -> none  [the longest x1 48.1 us: per_device(): lax.all_gather(density, 'tile', axis=0, tiled=True)]
    pallas_call x0 -> x3, Pallas kernels: none -> 77.6 us  [the longest x1 43.2 us: scatter(): pl.pallas_call(scatter_kernel, out_shape=(shape, shape), in_specs=[vmem]...]
    psum x1 -> x0, waiting for transfers between devices: 72.3 us -> none  [per_device(): bulk_sum, buoy_sum = lax.psum((own_bulk, own_buoy), 'grp')]
    add x11 -> x0, other arithmetic: 39.3 us -> none  [the longest x1 14.3 us: evolve(): bulk_image = bulk_image + changes[step_index][0] * adj_pressure]
    all_gather x1 -> x0, blocking collectives: 29 us -> none  [per_device(): lists = lax.all_gather(aperture, 'tile', axis=0, tiled=True)]
    dot_general x6 -> x0, matrix products: 17.3 us -> none  [the longest x1 6 us: per_device(): ap_speed = jnp.einsum('jt,txyz->jxyz', select, pieces[0], precision=highest)]
    all_to_all x2 -> x0, starting transfers between devices: 12.3 us -> none  [the longest x1 6.43 us: per_device(): lax.all_to_all(back_buoy, 'tile', split_axis=0, concat_axis=0, tiled=True)]
    all_to_all x2 -> x0, waiting for transfers between devices: 11.9 us -> none  [the longest x1 11.9 us: per_device(): lax.all_to_all(back_bulk, 'tile', split_axis=0, concat_axis=0, tiled=True)]
  transfers between devices with their start and end apart: 5 -> 0, of which waited for: 4 -> 0; matrix products, arithmetic and copies ran while one was open for 6% -> 0% of each run, Pallas kernels for 0% -> 0%
where the time goes in v1:
time: 89.7 us; the launch traced here: 88.3 us
  Pallas kernels  77.6 us (87%)
  local copies, waits for them, and re-layouts  9.99 us (11%)
    pallas_call x1, Pallas kernels, scatter(): pl.pallas_call(scatter_kernel, out_shape=(shape, shape), in_specs=[vmem]...  43.2 us
    pallas_call x1, Pallas kernels, gather(): pl.pallas_call(gather_kernel, out_shape=(jax.ShapeDtypeStruct((2, 8, FIEL...  23.4 us
    pallas_call x1, Pallas kernels, evolve(): pl.pallas_call(evolve_kernel, out_shape=jax.ShapeDtypeStruct((16, 2, 2 *...  10.9 us
    unnamed x33, local copies, waits for them, and re-layouts  9.81 us

profile of v1, /device:TPU:2, one launch (start us, length us, event | category | flops | bytes accessed | tf_op | source)
XLA Modules:
  0.0 88.3 jit_solution(2363064469088200853)
XLA Ops:
  0.6 0.0 copy-start.13
  0.6 0.7 copy-done.13
  1.3 0.0 copy-start.14
  1.3 0.1 reshape.43.resid
  1.4 0.6 copy-done.14
  2.0 0.1 copy.16
  2.1 0.0 copy-start.10
  2.1 0.1 reshape.42.recs
  2.2 0.5 copy-done.10
  2.7 0.0 copy-start.2
  2.7 0.9 %copy-done.2 = f32[4,2,32,128]{3,2,1,0:T(8,128)S(1)} copy-done((f32[4,2,32,128]{3,2,1,0:T(8,128)S(1)}, f32[4,2,32,128]{3,2,1,0:T(8,128)}, u32[]{:S(2)}) %copy-start.2) | copy-done | bytes 131096
  3.6 0.0 copy-start.4
  3.6 0.9 %copy-done.4 = f32[4,2,32,128]{3,2,1,0:T(8,128)S(1)} copy-done((f32[4,2,32,128]{3,2,1,0:T(8,128)S(1)}, f32[4,2,32,128]{3,2,1,0:T(8,128)}, u32[]{:S(2)}) %copy-start.4) | copy-done | bytes 131096
  4.5 0.0 copy-start.6
  4.5 0.0 copy-start.7
  4.5 23.4 %shard_map.140 = (f32[2,8,2,8,8,128]{5,4,3,2,1,0:T(8,128)S(1)}, s32[8,8,128]{2,1,0:T(8,128)S(1)}) custom-call(s32[1,16]{1,0:T(1,128)S(1)} %copy-done.10, f32[4,8,8,128]{3,2,1,0:T(8,128)S(1)} %bitcast.14, f32[4,8,8,128]{3,2,1,0:T(8,128)S(1)} %bitcast.16), custom_call_target="tpu_custom_call" | custom-call | flops 1000000 | bytes 62914560 | tf_op jit(solution)/shard_map/pallas_call | solution.py:311
  28.0 0.0 copy-start.11
  28.0 0.0 copy-start.12
  28.0 0.0 copy-done.6
  28.0 0.0 copy-done.7
  28.0 0.6 copy-done.11
  28.7 0.0 copy-done.12
  28.7 0.0 copy-start
  28.7 1.2 %copy-done = bf16[1,4,32,32,128]{4,3,2,1,0:T(8,128)(2,1)S(1)} copy-done((bf16[1,4,32,32,128]{4,3,2,1,0:T(8,128)(2,1)S(1)}, bf16[1,4,32,32,128]{4,3,2,1,0:T(8,128)(2,1)}, u32[]{:S(2)}) %copy-start) | copy-done | bytes 1048600
  29.9 0.0 copy-start.1
  29.9 1.2 %copy-done.1 = bf16[1,4,32,32,128]{4,3,2,1,0:T(8,128)(2,1)S(1)} copy-done((bf16[1,4,32,32,128]{4,3,2,1,0:T(8,128)(2,1)S(1)}, bf16[1,4,32,32,128]{4,3,2,1,0:T(8,128)(2,1)}, u32[]{:S(2)}) %copy-start.1) | copy-done | bytes 1048600
  31.1 0.0 copy-start.8
  31.1 0.8 copy-done.8
  32.0 0.0 copy-start.9
  32.0 0.8 copy-done.9
  32.8 0.0 copy-start.3
  32.8 0.0 copy-start.5
  32.8 10.9 %shard_map.141 = f32[16,2,64,128]{3,2,1,0:T(8,128)S(1)} custom-call(s32[1,16]{1,0:T(1,128)S(1)} %copy-done.10, s32[1,3]{1,0:T(1,128)S(1)} %copy-done.11, f32[1,4]{1,0:T(1,128)S(1)} %copy-done.12, s32[1,64]{1,0:T(1,128)S(1)} %reshape.42.recs, f32[1,128]{1,0:T(1,128)S(1)} %reshape.43.resid, bf16[256,256]{1,0:T(8,128)(2,1)S(1)} %copy-done.7, ...), custom_call_target="tpu_custom_call" | custom-call | flops 1000000000 | bytes 5242880 | tf_op jit(solution)/shard_map/pallas_call | solution.py:170
  43.7 0.0 copy-done.3
  43.7 0.0 copy-done.5
  43.7 43.2 %shard_map.142 = (f32[8,4,8,128]{3,2,1,0:T(8,128)S(1)}, f32[8,4,8,128]{3,2,1,0:T(8,128)S(1)}) custom-call(s32[8,8,128]{2,1,0:T(8,128)S(1)} %get-tuple-element.6.codes, f32[2,8,2,8,8,128]{5,4,3,2,1,0:T(8,128)S(1)} %bitcast.10, f32[8,4,8,128]{3,2,1,0:T(8,128)S(1)} %bitcast.15, f32[8,4,8,128]{3,2,1,0:T(8,128)S(1)} %bitcast.17), custom_call_target="tpu_custom_call" | custom-call | flops 1000000 | bytes 62914560 | tf_op jit(solution)/shard_map/pallas_call | solution.py:444
  87.0 0.7 copy.19
  87.6 0.7 copy.20
Async XLA Ops:
  0.6 0.7 copy-start.13
  1.3 0.7 copy-start.14
  2.1 0.7 copy-start.10
  2.7 0.9 %copy-start.2 = (f32[4,2,32,128]{3,2,1,0:T(8,128)S(1)}, f32[4,2,32,128]{3,2,1,0:T(8,128)}, u32[]{:S(2)}) copy-start(f32[4,2,32,128]{3,2,1,0:T(8,128)} %param.13) | copy-start | bytes 393220
  3.6 0.9 %copy-start.4 = (f32[4,2,32,128]{3,2,1,0:T(8,128)S(1)}, f32[4,2,32,128]{3,2,1,0:T(8,128)}, u32[]{:S(2)}) copy-start(f32[4,2,32,128]{3,2,1,0:T(8,128)} %param.14) | copy-start | bytes 393220
  4.5 23.5 %copy-start.6 = (bf16[256,256]{1,0:T(8,128)(2,1)S(1)}, bf16[256,256]{1,0:T(8,128)(2,1)}, u32[]{:S(2)}) copy-start(bf16[256,256]{1,0:T(8,128)(2,1)} %constant.9.clone.yminus_ref) | copy-start | bytes 393220
  4.5 23.5 %copy-start.7 = (bf16[256,256]{1,0:T(8,128)(2,1)S(1)}, bf16[256,256]{1,0:T(8,128)(2,1)}, u32[]{:S(2)}) copy-start(bf16[256,256]{1,0:T(8,128)(2,1)} %constant.8.clone.yplus_ref) | copy-start | bytes 393220
  28.0 0.7 copy-start.11
  28.0 0.7 copy-start.12
  28.7 1.2 %copy-start = (bf16[1,4,32,32,128]{4,3,2,1,0:T(8,128)(2,1)S(1)}, bf16[1,4,32,32,128]{4,3,2,1,0:T(8,128)(2,1)}, u32[]{:S(2)}) copy-start(bf16[1,4,32,32,128]{4,3,2,1,0:T(8,128)(2,1)} %param.15) | copy-start | bytes 3145732
  29.9 1.2 %copy-start.1 = (bf16[1,4,32,32,128]{4,3,2,1,0:T(8,128)(2,1)S(1)}, bf16[1,4,32,32,128]{4,3,2,1,0:T(8,128)(2,1)}, u32[]{:S(2)}) copy-start(bf16[1,4,32,32,128]{4,3,2,1,0:T(8,128)(2,1)} %param.16) | copy-start | bytes 3145732
  31.1 0.8 copy-start.8
  32.0 0.8 copy-start.9
  32.8 10.9 %copy-start.3 = (f32[4,2,32,128]{3,2,1,0:T(8,128)S(1)}, f32[4,2,32,128]{3,2,1,0:T(8,128)}, u32[]{:S(2)}) copy-start(f32[4,2,32,128]{3,2,1,0:T(8,128)} %param.13) | copy-start | bytes 393220
  32.8 10.9 %copy-start.5 = (f32[4,2,32,128]{3,2,1,0:T(8,128)S(1)}, f32[4,2,32,128]{3,2,1,0:T(8,128)}, u32[]{:S(2)}) copy-start(f32[4,2,32,128]{3,2,1,0:T(8,128)} %param.14) | copy-start | bytes 393220

commit v2 on v1

v2 whole, which is shorter than its diff:
```python
import math

import jax
import jax.numpy as jnp
import numpy as np
from jax import lax
from jax.experimental import pallas as pl
from jax.experimental.pallas import tpu as pltpu
from jax.sharding import PartitionSpec as P

COEF = (1225.0 / 1024.0, -245.0 / 3072.0, 49.0 / 5120.0, -5.0 / 7168.0)
SCALE = COEF[0] / (165.0 / 128.0)
TAPS = tuple(np.asarray(np.array(COEF) / SCALE, dtype=jnp.bfloat16).astype(np.float64).tolist())
STEPS = 4
NX, NY, NZ = 32, 32, 128
GROUP = 8 * NY
GROUPS = NX // 8
PAD = 4 * NY
CELLS = NX * NY


def difference_matrix(size, blocks):
    plus = np.zeros((size, size))
    for k in range(1, 5):
        plus += TAPS[k - 1] * (np.eye(size, k=k) - np.eye(size, k=1 - k))
    return np.kron(np.eye(blocks), plus)


def split(values):
    high = values.astype(jnp.bfloat16)
    low = (values - high.astype(jnp.float32)).astype(jnp.bfloat16)
    return jnp.concatenate([high, low], axis=1)


def along_y(matrix, parts):
    both = jnp.dot(matrix, parts, preferred_element_type=jnp.float32)
    return both[:, :NZ] + both[:, NZ:]


def along_z(parts, matrix):
    return jnp.dot(parts, matrix, preferred_element_type=jnp.float32)


def along_x(ref, base, backward):
    def plane(k):
        return ref[pl.ds(base + PAD + (k - backward) * NY, GROUP), :]

    total = None
    for k in range(1, 5):
        term = TAPS[k - 1] * (plane(k) - plane(1 - k))
        total = term if total is None else total + term
    return total


MESH = pl.DeviceIdType.MESH
FIELDS = 2
TILES = 4


def place():
    tile = lax.axis_index("tile")
    return tile // 8, lax.rem(tile // 2, 4), lax.rem(tile, 2)


def tile_at(x, y, core):
    return lax.rem(x + 4, 4) * 8 + lax.rem(y + 4, 4) * 2 + lax.rem(core, 2)


def remote(source, target, send, receive, device):
    return pltpu.make_async_remote_copy(
        src_ref=source, dst_ref=target, send_sem=send, recv_sem=receive,
        device_id=device, device_id_type=MESH,
    )


def greet(devices):
    barrier = pltpu.get_barrier_semaphore()
    for device in devices:
        pl.semaphore_signal(barrier, inc=1, device_id=device, device_id_type=MESH)
    return lambda: pl.semaphore_wait(barrier, len(devices))


def matches(code, residue):
    corner, level = code >> 2, code & 3
    upper = corner > residue
    return [
        [jnp.logical_and(level == t, upper if high else jnp.logical_not(upper)) for t in range(TILES)]
        for high in range(2)
    ]


ORDER = (2, 3, 6, 7, 4, 5, 1)


def kernel(
    ap, src, wave, recs, resid, speed_in, density_in, fwd_in, adj_in, yplus_in, yminus_in, zplus_in, zminus_in,
    grad_speed, grad_density,
    speed, density, fwd, adj, yplus, yminus, zplus, zminus, in_sems,
    row, staged, bulk_tiles, buoy_tiles, codes, x_send, x_recv, c_send, c_recv, y_send, y_recv,
    pres, vel0, vel1, vel2, apres, avel0, avel1, avel2, bulk, buoy, dpres, dvel, bulk_image, buoy_image,
    image, came, part, passed, summed, total, terms,
    iy_send, iy_recv, ix_send, ix_recv, z_send, z_recv, g_send, g_recv,
):
    z = lax.axis_index("grp")
    x, y, core = place()
    right, left = {"tile": tile_at(x + 1, y, core)}, {"tile": tile_at(x - 1, y, core)}
    ahead = [{"tile": tile_at(x, y + j // 2, core + j % 2)} for j in range(8)]
    back = [{"tile": tile_at(x, y - j // 2, core + j % 2)} for j in range(8)]
    column = [{"grp": lax.rem(z + d, 8)} for d in range(8)]
    ready = greet([right, left] + ahead[1:] + column[1:])
    loads = [
        pltpu.make_async_copy(source, target, in_sems.at[i])
        for i, (source, target) in enumerate(
            (
                (density_in, density), (speed_in, speed), (fwd_in, fwd), (adj_in, adj),
                (yplus_in, yplus), (zplus_in, zplus), (yminus_in, yminus), (zminus_in, zminus),
            )
        )
    ]
    for load in loads:
        load.start()
    codes[0] = jnp.zeros((8, NZ), jnp.int32) + ap[0, 0]
    loads[0].wait()
    loads[1].wait()
    for t in range(TILES):
        dense = density[t]
        row[1, x, t] = 1.0 / dense
    for t in range(TILES):
        dense, fast = density[t], speed[t]
        row[0, x, t] = dense * fast * fast
    models, images = (bulk_tiles, buoy_tiles), (bulk_image, buoy_image)
    xl, xr, x2 = lax.rem(x + 3, 4), lax.rem(x + 1, 4), lax.rem(x + 2, 4)
    other, same = lax.rem(x + 1, 2), lax.rem(x, 2)
    mine = y * 2 + core
    pending = []

    def start(copy):
        copy.start()
        pending.append(copy)

    ready()
    for f in (1, 0):
        for side, device in ((0, right), (1, left)):
            start(remote(row.at[f, x], row.at[f, x], x_send.at[0, side, f], x_recv.at[0, side, f], device))
        if f == 1:
            for j in range(1, 8):
                start(remote(codes.at[0], codes.at[j], c_send.at[j], c_recv.at[j], ahead[j]))

    edge = jnp.zeros((PAD, NZ), jnp.float32)
    for ref in (pres, vel0, apres, avel0):
        ref[0:PAD, :] = edge
        ref[PAD + CELLS :, :] = edge
    forward_refs = (pres, vel0, vel1, vel2)
    adjoint_refs = (apres, avel0, avel1, avel2)

    def rows_of(g):
        return pl.ds(g * GROUP, GROUP)

    def padded_of(g):
        return pl.ds(PAD + g * GROUP, GROUP)

    def spots(g):
        return (padded_of(g), padded_of(g), rows_of(g), rows_of(g))

    def unpack(state, refs):
        for g in range(GROUPS):
            for i, (ref, spot) in enumerate(zip(refs, spots(g))):
                ref[spot, :] = state[0, i, rows_of(g), :].astype(jnp.float32)

    def differences(ref, g):
        parts = split(ref[padded_of(g), :])
        return (
            along_x(ref, g * GROUP, 0),
            along_y(yplus[...], parts),
            along_z(parts, zplus[...]),
        )

    def divergence(refs, g):
        return (
            along_x(refs[1], g * GROUP, 1)
            + along_y(yminus[...], split(refs[2][rows_of(g), :]))
            + along_z(split(refs[3][rows_of(g), :]), zminus[...])
        )

    cell = lax.broadcasted_iota(jnp.int32, (NY, NZ), 0) * NZ + lax.broadcasted_iota(jnp.int32, (NY, NZ), 1)
    fired = (src[0, 0] * NY + src[0, 1]) * NZ + src[0, 2]

    def source(n, g):
        planes = []
        for i in range(8):
            planes.append(jnp.where(cell == fired - (g * 8 + i) * NY * NZ, wave[0, n], 0.0))
        return jnp.concatenate(planes, axis=0)

    def received(n, g):
        planes = []
        for i in range(8):
            j = g * 8 + i
            planes.append(jnp.where(cell == recs[0, 0, j] * NZ + recs[0, 1, j], resid[0, n, j], 0.0))
        return jnp.concatenate(planes, axis=0)

    for load in loads[2:]:
        load.wait()
    for state, refs, slot in ((fwd, forward_refs, 0), (adj, adjoint_refs, 1)):
        unpack(state, refs)
        for g in range(GROUPS):
            for d, values in enumerate(differences(refs[0], g)):
                dvel[slot, d, rows_of(g), :] = values

    def forward(f):
        for side, device, origin in ((0, right, xl), (1, left, xr)):
            whole = row.at[f, origin]
            remote(whole, whole, x_send.at[0, side, f], x_recv.at[0, side, f], device).wait_recv()
            half = row.at[f, origin, pl.ds(2 * side, 2)]
            start(remote(half, half, x_send.at[1, side, f], x_recv.at[1, side, f], device))

    def passed_on(f):
        for side, device in ((0, right), (1, left)):
            half = row.at[f, x2, pl.ds(2 * side, 2)]
            remote(half, half, x_send.at[1, side, f], x_recv.at[1, side, f], device).wait_recv()

    def select(code, parity, f):
        found = matches(code, parity * 8 + mine)
        chosen = jnp.zeros((8, 8, NZ), jnp.float32)
        for high in range(2):
            for t in range(TILES):
                chosen = jnp.where(found[high][t][None], row[f, parity + 2 * high, t], chosen)
        return chosen

    def serve(parity, own, f):
        for j in ORDER:
            if own == 0 and f == 1:
                remote(codes.at[0], codes.at[j], c_send.at[j], c_recv.at[j], ahead[j]).wait_recv()
            staged[own, f, j] = select(codes[j], parity, f)
            start(
                remote(
                    staged.at[own, f, j], models[f].at[parity * 8 + mine],
                    y_send.at[own, f, j], y_recv.at[own, f, j], back[j],
                )
            )
        models[f][parity * 8 + mine] = select(codes[0], parity, f)

    def arrived(f):
        for own, parity in ((0, other), (1, same)):
            for j in range(1, 8):
                origin = lax.rem(y + j // 2, 4) * 2 + lax.rem(core + j % 2, 2)
                remote(
                    staged.at[own, f, j], models[f].at[parity * 8 + origin],
                    y_send.at[own, f, j], y_recv.at[own, f, j], back[j],
                ).wait_recv()

    forward(1)
    serve(other, 0, 1)
    passed_on(1)
    serve(same, 1, 1)
    forward(0)
    serve(other, 0, 0)
    passed_on(0)
    serve(same, 1, 0)

    corner = ap[0, 0] >> 2

    def place_model(f, ref):
        for j in range(16):
            values = models[f][(corner + j) & 15]
            ref[pl.ds(j * 2 * NY, 2 * NY), :] = SCALE * values.reshape(2 * NY, NZ)

    arrived(1)
    place_model(1, buoy)
    for g in range(GROUPS):
        light = buoy[rows_of(g), :]
        for d in range(3):
            spot = spots(g)[1 + d]
            change = light * dvel[0, d, rows_of(g), :]
            dvel[0, d, rows_of(g), :] = change
            forward_refs[1 + d][spot, :] += change
            adjoint_refs[1 + d][spot, :] += light * dvel[1, d, rows_of(g), :]
    for g in range(GROUPS):
        dpres[0, rows_of(g), :] = divergence(forward_refs, g)
        dpres[1, rows_of(g), :] = divergence(adjoint_refs, g)
    arrived(0)
    place_model(0, bulk)
    for g in range(GROUPS):
        stiff = bulk[rows_of(g), :]
        change = stiff * dpres[0, rows_of(g), :] + source(0, g)
        dpres[0, rows_of(g), :] = change
        pres[padded_of(g), :] += change
        apres[padded_of(g), :] += stiff * dpres[1, rows_of(g), :] + received(STEPS - 1, g)

    def move(refs, g):
        light = buoy[rows_of(g), :]
        changes, moved = [], []
        for d, values in enumerate(differences(refs[0], g)):
            change = light * values
            after = refs[1 + d][spots(g)[1 + d], :] + change
            refs[1 + d][spots(g)[1 + d], :] = after
            changes.append(change)
            moved.append(after)
        return changes, moved

    def set_image(f, g, values):
        images[f][4 * g : 4 * g + 4] = values.reshape(4, 2 * NY, NZ)

    def get_image(f, g):
        return images[f][4 * g : 4 * g + 4].reshape(GROUP, NZ)

    def inner(changes, others):
        return changes[0] * others[0] + changes[1] * others[1] + changes[2] * others[2]

    def replay(n, carry):
        for g in range(GROUPS):
            changes, _ = move(forward_refs, g)
            for d in range(3):
                dvel[n, d, rows_of(g), :] = changes[d]
        for g in range(GROUPS):
            change = bulk[rows_of(g), :] * divergence(forward_refs, g) + source(n, g)
            dpres[n, rows_of(g), :] = change
            pres[padded_of(g), :] += change
        return carry

    lax.fori_loop(1, STEPS - 1, replay, 0)
    for g in range(GROUPS):
        changes, _ = move(forward_refs, g)
        set_image(1, g, inner(changes, [adjoint_refs[1 + d][spots(g)[1 + d], :] for d in range(3)]))
    for g in range(GROUPS):
        change = bulk[rows_of(g), :] * divergence(forward_refs, g) + source(STEPS - 1, g)
        set_image(0, g, change * apres[padded_of(g), :])

    def adjoint_velocities(n):
        for g in range(GROUPS):
            _, moved = move(adjoint_refs, g)
            set_image(1, g, get_image(1, g) + inner([dvel[n, d, rows_of(g), :] for d in range(3)], moved))

    def adjoint_pressure(n):
        for g in range(GROUPS):
            after = (
                apres[padded_of(g), :]
                + bulk[rows_of(g), :] * divergence(adjoint_refs, g)
                + received(n, g)
            )
            apres[padded_of(g), :] = after
            set_image(0, g, get_image(0, g) + dpres[n, rows_of(g), :] * after)

    def back_step(i, carry):
        adjoint_velocities(STEPS - 2 - i)
        adjoint_pressure(STEPS - 2 - i)
        return carry

    lax.fori_loop(0, STEPS - 2, back_step, 0)

    def image_copy(own, parity, f, j):
        target = lax.rem(y + j // 2, 4) * 2 + lax.rem(core + j % 2, 2)
        return remote(
            image.at[f, parity * 8 + target], came.at[own, f, j], iy_send.at[own, f, j], iy_recv.at[own, f, j], ahead[j]
        )

    def send_image(f):
        for r in range(16):
            image[f, r] = images[f][(r + 16 - corner) & 15].reshape(8, 8, NZ)
        for own, parity in ((1, same), (0, other)):
            for j in ORDER:
                start(image_copy(own, parity, f, j))

    def collect(own, parity, f):
        for j in range(1, 8):
            image_copy(own, parity, f, j).wait_recv()
        found = [matches(codes[j], parity * 8 + mine) for j in range(8)]
        for high in range(2):
            for t in range(TILES):
                held = None
                for j in range(8):
                    values = image[f, parity * 8 + mine] if j == 0 else came[own, f, j]
                    term = jnp.where(found[j][high][t][None], values, 0.0)
                    held = term if held is None else held + term
                part[f, parity + 2 * high, t] = held

    def hop(stage, side, f):
        device, target = ((right, xr), (left, xl))[side]
        if stage == 0:
            return remote(
                part.at[f, x2, pl.ds(2 * side, 2)], passed.at[side, f],
                ix_send.at[0, side, f], ix_recv.at[0, side, f], device,
            )
        return remote(
            part.at[f, target], summed.at[side, f], ix_send.at[1, side, f], ix_recv.at[1, side, f], device
        )

    def piece_copy(f, d):
        return remote(
            total.at[f, lax.rem(z + d, 8)], terms.at[f, d], z_send.at[f, d], z_recv.at[f, d], column[d]
        )

    def send_on(f):
        for side in range(2):
            target = (xr, xl)[side]
            hop(0, side, f).wait_recv()
            for i in range(2):
                part[f, target, 2 * side + i] += passed[side, f, i]
            start(hop(1, side, f))

    def send_pieces(f):
        for side in range(2):
            hop(1, side, f).wait_recv()
        for t in range(TILES):
            whole = part[f, x, t] + summed[0, f, t] + summed[1, f, t]
            total[f, 2 * t] = whole[:4]
            total[f, 2 * t + 1] = whole[4:]
        for d in (4, 3, 5, 2, 6, 1, 7):
            start(piece_copy(f, d))

    def collect_same(f):
        collect(1, same, f)
        for side in range(2):
            start(hop(0, side, f))

    def collect_other(f):
        collect(0, other, f)
        send_on(f)

    adjoint_velocities(0)
    send_image(1)
    adjoint_pressure(0)
    send_image(0)
    collect_same(1)
    collect_other(1)
    collect_same(0)
    send_pieces(1)
    collect_other(0)
    send_pieces(0)
    sums = []
    for f in range(FIELDS):
        whole = total[f, z]
        for d in range(1, 8):
            piece_copy(f, d).wait_recv()
            whole = whole + terms[f, d]
        sums.append(whole)
    half = pl.ds(4 * lax.rem(z, 2), 4)
    fast, dense = speed[z // 2, half], density[z // 2, half]
    factor = 1.0 / math.sqrt(256.0)
    grad_speed[z] = factor * (sums[0] * (2.0 * dense * fast))
    grad_density[z] = factor * (sums[0] * (fast * fast) - sums[1] / (dense * dense))

    def result_copy(i, d, piece):
        ref = (grad_speed, grad_density)[i]
        return remote(ref.at[piece], ref.at[piece], g_send.at[i, d], g_recv.at[i, d], column[d])

    for d in (4, 3, 5, 2, 6, 1, 7):
        for i in range(2):
            start(result_copy(i, d, z))
    for d in range(1, 8):
        for i in range(2):
            result_copy(i, d, lax.rem(z + 8 - d, 8)).wait_recv()
    for copy in pending:
        copy.wait_send()


def per_device(speed, density, fwd_state, adj_state, aperture, src_pos, wavelet, rec_pos, residual):
    yplus = difference_matrix(NY, 8)
    zplus = difference_matrix(NZ, 1)
    matrices = [
        jnp.asarray(m, jnp.bfloat16)
        for m in (yplus, -yplus.T, np.concatenate([zplus.T, zplus.T]), np.concatenate([-zplus, -zplus]))
    ]
    smem = pl.BlockSpec(memory_space=pltpu.SMEM)
    vmem = pl.BlockSpec(memory_space=pltpu.VMEM)
    whole = pl.BlockSpec(memory_space=pl.ANY)
    dma = pltpu.SemaphoreType.DMA

    def floats(*shape):
        return pltpu.VMEM(shape + (NZ,), jnp.float32)

    def halves(*shape):
        return pltpu.VMEM(shape, jnp.bfloat16)

    tiles = floats(TILES, 8, 8)
    field, wide = floats(CELLS), floats(CELLS + 2 * PAD)
    shape = jax.ShapeDtypeStruct((8, 4, 8, NZ), jnp.float32)
    grads = pl.pallas_call(
        kernel,
        out_shape=(shape, shape),
        in_specs=[smem] * 5 + [whole] * 8,
        out_specs=(vmem, vmem),
        scratch_shapes=[
            tiles, tiles, halves(1, 4, CELLS, NZ), halves(1, 4, CELLS, NZ),
            halves(GROUP, GROUP), halves(GROUP, GROUP), halves(2 * NZ, NZ), halves(2 * NZ, NZ), dma((8,)),
            floats(FIELDS, 4, TILES, 8, 8), floats(2, FIELDS, 8, 8, 8), floats(16, 8, 8), floats(16, 8, 8),
            pltpu.VMEM((8, 8, NZ), jnp.int32),
            dma((2, 2, FIELDS)), dma((2, 2, FIELDS)), dma((8,)), dma((8,)), dma((2, FIELDS, 8)), dma((2, FIELDS, 8)),
            wide, wide, field, field, wide, wide, field, field, field, field,
            floats(STEPS - 1, CELLS), floats(STEPS - 1, 3, CELLS), floats(16, 2 * NY), floats(16, 2 * NY),
            floats(FIELDS, 16, 8, 8), floats(2, FIELDS, 8, 8, 8), floats(FIELDS, 4, TILES, 8, 8),
            floats(2, FIELDS, 2, 8, 8), floats(2, FIELDS, TILES, 8, 8),
            floats(FIELDS, 8, 4, 8), floats(FIELDS, 8, 4, 8),
            dma((2, FIELDS, 8)), dma((2, FIELDS, 8)), dma((2, 2, FIELDS)), dma((2, 2, FIELDS)),
            dma((FIELDS, 8)), dma((FIELDS, 8)), dma((2, 8)), dma((2, 8)),
        ],
        compiler_params=pltpu.CompilerParams(
            collective_id=0, has_side_effects=True, vmem_limit_bytes=56 * 1024 * 1024
        ),
    )(
        aperture, src_pos, wavelet, rec_pos.transpose(0, 2, 1), residual,
        speed.reshape(TILES, 8, 8, NZ), density.reshape(TILES, 8, 8, NZ),
        fwd_state.reshape(1, 4, CELLS, NZ), adj_state.reshape(1, 4, CELLS, NZ), *matrices,
    )
    return tuple(grad.reshape(speed.shape) for grad in grads)


def solution(mesh):
    return jax.shard_map(
        per_device,
        mesh=mesh,
        in_specs=(
            P("tile", None, None, None),
            P("tile", None, None, None),
            P(("grp", "tile"), None, None, None, None),
            P(("grp", "tile"), None, None, None, None),
            P(("grp", "tile"), None),
            P(("grp", "tile"), None),
            P(("grp", "tile"), None),
            P(("grp", "tile"), None, None),
            P(("grp", "tile"), None, None),
        ),
        out_specs=(P("tile", None, None, None), P("tile", None, None, None)),
        check_vma=False,
    )
```

time: 89.7 us -> 72.9 us (0.81); the launches traced: 88.3 us -> 72.8 us
  local copies, waits for them, and re-layouts: 9.99 us -> 2.26 us
  Pallas kernels: 77.6 us -> 69.9 us
    pallas_call x3 -> x1, Pallas kernels: 77.6 us -> 69.9 us  [per_device(): pl.pallas_call(kernel, out_shape=(shape, shape), in_specs=[smem] * 5 + [w...]
    unnamed x33 -> x4, local copies, waits for them, and re-layouts: 9.81 us -> 2.26 us
where the time goes in v2:
time: 72.9 us; the launch traced here: 72.8 us
  Pallas kernels  69.9 us (96%)
  local copies, waits for them, and re-layouts  2.26 us (3%)
    pallas_call x1, Pallas kernels, per_device(): pl.pallas_call(kernel, out_shape=(shape, shape), in_specs=[smem] * 5 + [w...  69.9 us
    unnamed x4, local copies, waits for them, and re-layouts  2.26 us

profile of v2, /device:TPU:2, one launch (start us, length us, event | category | flops | bytes accessed | tf_op | source)
XLA Modules:
  0.0 72.8 jit_solution(9660412698259239140)
XLA Ops:
  0.6 69.9 %shard_map.140 = (f32[8,4,8,128]{3,2,1,0:T(8,128)}, f32[8,4,8,128]{3,2,1,0:T(8,128)}) custom-call(s32[1,16]{1,0:T(1,128)} %ap.1, s32[1,3]{1,0:T(1,128)} %src.1, f32[1,4]{1,0:T(1,128)} %wave.1, s32[1,2,32]{2,1,0:T(2,128)} %bitcast.13, f32[1,4,32]{2,1,0:T(4,128)} %resid.1, f32[4,8,8,128]{3,2,1,0:T(8,128)} %bitcast.9, f32[4,8,8,128]{3,2,1,0:T(8,128)} %bitcast.10, ...), custom_call_target="tpu_custom_call" | custom-call | tf_op jit(solution)/shard_map/pallas_call | solution.py:477
  70.5 0.0 copy-start
  70.5 1.6 %copy.17 = f32[4,2,32,128]{3,2,1,0:T(8,128)} copy(f32[4,2,32,128]{3,2,1,0:T(8,128)} %bitcast.12) | data formatting | bytes 262144
  72.1 0.0 copy-done
  72.1 0.7 copy.18
Async XLA Ops:
  70.5 1.6 %copy-start = (f32[8,4,8,128]{3,2,1,0:T(8,128)S(1)}, f32[8,4,8,128]{3,2,1,0:T(8,128)}, u32[]{:S(2)}) copy-start(f32[8,4,8,128]{3,2,1,0:T(8,128)} %get-tuple-element.5) | copy-start | bytes 393220

commit v3 on v2

--- a/solution.py
+++ b/solution.py
@@ -54,6 +54,7 @@
 
 MESH = pl.DeviceIdType.MESH
 FIELDS = 2
+HALVES = 2
 TILES = 4
 
 
@@ -89,7 +90,8 @@
     ]
 
 
-ORDER = (2, 3, 6, 7, 4, 5, 1)
+ORDER = (4, 5, 2, 3, 6, 7, 1)
+FAR = (4, 3, 5, 2, 6, 1, 7)
 
 
 def kernel(
@@ -98,7 +100,7 @@
     speed, density, fwd, adj, yplus, yminus, zplus, zminus, in_sems,
     row, staged, bulk_tiles, buoy_tiles, codes, x_send, x_recv, c_send, c_recv, y_send, y_recv,
     pres, vel0, vel1, vel2, apres, avel0, avel1, avel2, bulk, buoy, dpres, dvel, bulk_image, buoy_image,
-    image, came, part, passed, summed, total, terms,
+    image, came, part, passed, summed, total, terms, sums,
     iy_send, iy_recv, ix_send, ix_recv, z_send, z_recv, g_send, g_recv,
 ):
     z = lax.axis_index("grp")
@@ -138,10 +140,18 @@
         copy.start()
         pending.append(copy)
 
+    def row_copy(f, side, origin):
+        part = row.at[f, origin]
+        return remote(part, part, x_send.at[0, side, f], x_recv.at[0, side, f], (right, left)[side])
+
+    def half_copy(f, side, origin):
+        part = row.at[f, origin, pl.ds(2 * side, 2)]
+        return remote(part, part, x_send.at[1, side, f], x_recv.at[1, side, f], (right, left)[side])
+
     ready()
     for f in (1, 0):
-        for side, device in ((0, right), (1, left)):
-            start(remote(row.at[f, x], row.at[f, x], x_send.at[0, side, f], x_recv.at[0, side, f], device))
+        for side in range(2):
+            start(row_copy(f, side, x))
         if f == 1:
             for j in range(1, 8):
                 start(remote(codes.at[0], codes.at[j], c_send.at[j], c_recv.at[j], ahead[j]))
@@ -206,18 +216,6 @@
             for d, values in enumerate(differences(refs[0], g)):
                 dvel[slot, d, rows_of(g), :] = values
 
-    def forward(f):
-        for side, device, origin in ((0, right, xl), (1, left, xr)):
-            whole = row.at[f, origin]
-            remote(whole, whole, x_send.at[0, side, f], x_recv.at[0, side, f], device).wait_recv()
-            half = row.at[f, origin, pl.ds(2 * side, 2)]
-            start(remote(half, half, x_send.at[1, side, f], x_recv.at[1, side, f], device))
-
-    def passed_on(f):
-        for side, device in ((0, right), (1, left)):
-            half = row.at[f, x2, pl.ds(2 * side, 2)]
-            remote(half, half, x_send.at[1, side, f], x_recv.at[1, side, f], device).wait_recv()
-
     def select(code, parity, f):
         found = matches(code, parity * 8 + mine)
         chosen = jnp.zeros((8, 8, NZ), jnp.float32)
@@ -226,36 +224,34 @@
                 chosen = jnp.where(found[high][t][None], row[f, parity + 2 * high, t], chosen)
         return chosen
 
+    def tile_copy(parity, own, f, j, origin):
+        return remote(
+            staged.at[own, f, j], models[f].at[parity * 8 + origin], y_send.at[own, f, j], y_recv.at[own, f, j], back[j]
+        )
+
     def serve(parity, own, f):
         for j in ORDER:
             if own == 0 and f == 1:
                 remote(codes.at[0], codes.at[j], c_send.at[j], c_recv.at[j], ahead[j]).wait_recv()
             staged[own, f, j] = select(codes[j], parity, f)
-            start(
-                remote(
-                    staged.at[own, f, j], models[f].at[parity * 8 + mine],
-                    y_send.at[own, f, j], y_recv.at[own, f, j], back[j],
-                )
-            )
+            start(tile_copy(parity, own, f, j, mine))
         models[f][parity * 8 + mine] = select(codes[0], parity, f)
 
     def arrived(f):
         for own, parity in ((0, other), (1, same)):
             for j in range(1, 8):
                 origin = lax.rem(y + j // 2, 4) * 2 + lax.rem(core + j % 2, 2)
-                remote(
-                    staged.at[own, f, j], models[f].at[parity * 8 + origin],
-                    y_send.at[own, f, j], y_recv.at[own, f, j], back[j],
-                ).wait_recv()
-
-    forward(1)
-    serve(other, 0, 1)
-    passed_on(1)
-    serve(same, 1, 1)
-    forward(0)
-    serve(other, 0, 0)
-    passed_on(0)
-    serve(same, 1, 0)
+                tile_copy(parity, own, f, j, origin).wait_recv()
+
+    for f in (1, 0):
+        for side, origin in ((0, xl), (1, xr)):
+            row_copy(f, side, origin).wait_recv()
+            start(half_copy(f, side, origin))
+        serve(other, 0, f)
+    for f in (1, 0):
+        for side in range(2):
+            half_copy(f, side, x2).wait_recv()
+        serve(same, 1, f)
 
     corner = ap[0, 0] >> 2
 
@@ -360,61 +356,73 @@
             for j in ORDER:
                 start(image_copy(own, parity, f, j))
 
-    def collect(own, parity, f):
-        for j in range(1, 8):
-            image_copy(own, parity, f, j).wait_recv()
+    def collect(own, parity, f, h):
+        if h == 0:
+            for j in range(1, 8):
+                image_copy(own, parity, f, j).wait_recv()
         found = [matches(codes[j], parity * 8 + mine) for j in range(8)]
+        rows = pl.ds(4 * h, 4)
         for high in range(2):
             for t in range(TILES):
                 held = None
                 for j in range(8):
-                    values = image[f, parity * 8 + mine] if j == 0 else came[own, f, j]
+                    values = image[f, parity * 8 + mine, rows] if j == 0 else came[own, f, j, rows]
                     term = jnp.where(found[j][high][t][None], values, 0.0)
                     held = term if held is None else held + term
-                part[f, parity + 2 * high, t] = held
-
-    def hop(stage, side, f):
+                part[f, h, parity + 2 * high, t] = held
+
+    def hop(stage, side, f, h):
         device, target = ((right, xr), (left, xl))[side]
         if stage == 0:
-            return remote(
-                part.at[f, x2, pl.ds(2 * side, 2)], passed.at[side, f],
-                ix_send.at[0, side, f], ix_recv.at[0, side, f], device,
-            )
+            origin, landing = part.at[f, h, x2, pl.ds(2 * side, 2)], passed.at[side, f, h]
+        else:
+            origin, landing = part.at[f, h, target], summed.at[side, f, h]
+        return remote(origin, landing, ix_send.at[stage, side, f, h], ix_recv.at[stage, side, f, h], device)
+
+    def collect_same(f):
+        for h in range(HALVES):
+            collect(1, same, f, h)
+            for side in range(2):
+                start(hop(0, side, f, h))
+
+    def collect_other(f):
+        for h in range(HALVES):
+            collect(0, other, f, h)
+            for side, target in ((0, xr), (1, xl)):
+                hop(0, side, f, h).wait_recv()
+                for i in range(2):
+                    part[f, h, target, 2 * side + i] += passed[side, f, h, i]
+                start(hop(1, side, f, h))
+
+    def piece_copy(f, h, d):
         return remote(
-            part.at[f, target], summed.at[side, f], ix_send.at[1, side, f], ix_recv.at[1, side, f], device
+            total.at[f, h, lax.rem(z + d, 8)], terms.at[f, h, d], z_send.at[f, h, d], z_recv.at[f, h, d], column[d]
         )
 
-    def piece_copy(f, d):
-        return remote(
-            total.at[f, lax.rem(z + d, 8)], terms.at[f, d], z_send.at[f, d], z_recv.at[f, d], column[d]
-        )
-
-    def send_on(f):
-        for side in range(2):
-            target = (xr, xl)[side]
-            hop(0, side, f).wait_recv()
-            for i in range(2):
-                part[f, target, 2 * side + i] += passed[side, f, i]
-            start(hop(1, side, f))
+    def result_copy(f, h, d, piece):
+        part_sum = sums.at[f, h, piece]
+        return remote(part_sum, part_sum, g_send.at[f, h, d], g_recv.at[f, h, d], column[d])
 
     def send_pieces(f):
-        for side in range(2):
-            hop(1, side, f).wait_recv()
-        for t in range(TILES):
-            whole = part[f, x, t] + summed[0, f, t] + summed[1, f, t]
-            total[f, 2 * t] = whole[:4]
-            total[f, 2 * t + 1] = whole[4:]
-        for d in (4, 3, 5, 2, 6, 1, 7):
-            start(piece_copy(f, d))
-
-    def collect_same(f):
-        collect(1, same, f)
-        for side in range(2):
-            start(hop(0, side, f))
-
-    def collect_other(f):
-        collect(0, other, f)
-        send_on(f)
+        for h in range(HALVES):
+            for side in range(2):
+                hop(1, side, f, h).wait_recv()
+            for t in range(TILES):
+                whole = part[f, h, x, t] + summed[0, f, h, t] + summed[1, f, h, t]
+                total[f, h, 2 * t] = whole[:2]
+                total[f, h, 2 * t + 1] = whole[2:]
+            for d in FAR:
+                start(piece_copy(f, h, d))
+
+    def finish_pieces(f):
+        for h in range(HALVES):
+            held = total[f, h, z]
+            for d in range(1, 8):
+                piece_copy(f, h, d).wait_recv()
+                held = held + terms[f, h, d]
+            sums[f, h, z] = held
+            for d in FAR:
+                start(result_copy(f, h, d, z))
 
     adjoint_velocities(0)
     send_image(1)
@@ -426,29 +434,19 @@
     send_pieces(1)
     collect_other(0)
     send_pieces(0)
-    sums = []
-    for f in range(FIELDS):
-        whole = total[f, z]
-        for d in range(1, 8):
-            piece_copy(f, d).wait_recv()
-            whole = whole + terms[f, d]
-        sums.append(whole)
-    half = pl.ds(4 * lax.rem(z, 2), 4)
-    fast, dense = speed[z // 2, half], density[z // 2, half]
-    factor = 1.0 / math.sqrt(256.0)
-    grad_speed[z] = factor * (sums[0] * (2.0 * dense * fast))
-    grad_density[z] = factor * (sums[0] * (fast * fast) - sums[1] / (dense * dense))
-
-    def result_copy(i, d, piece):
-        ref = (grad_speed, grad_density)[i]
-        return remote(ref.at[piece], ref.at[piece], g_send.at[i, d], g_recv.at[i, d], column[d])
-
-    for d in (4, 3, 5, 2, 6, 1, 7):
-        for i in range(2):
-            start(result_copy(i, d, z))
-    for d in range(1, 8):
-        for i in range(2):
-            result_copy(i, d, lax.rem(z + 8 - d, 8)).wait_recv()
+    finish_pieces(1)
+    finish_pieces(0)
+    for f in (1, 0):
+        for h in range(HALVES):
+            for d in range(1, 8):
+                result_copy(f, h, d, lax.rem(z + 8 - d, 8)).wait_recv()
+    for h in range(HALVES):
+        for piece in range(8):
+            t, spot = piece // 2, pl.ds(4 * h + 2 * (piece % 2), 2)
+            fast, dense = speed[t, spot], density[t, spot]
+            stiff, light = sums[0, h, piece], sums[1, h, piece]
+            grad_speed[t, spot] = stiff * (2.0 * dense * fast)
+            grad_density[t, spot] = stiff * (fast * fast) - light / (dense * dense)
     for copy in pending:
         copy.wait_send()
 
@@ -473,7 +471,7 @@
 
     tiles = floats(TILES, 8, 8)
     field, wide = floats(CELLS), floats(CELLS + 2 * PAD)
-    shape = jax.ShapeDtypeStruct((8, 4, 8, NZ), jnp.float32)
+    shape = jax.ShapeDtypeStruct((TILES, 8, 8, NZ), jnp.float32)
     grads = pl.pallas_call(
         kernel,
         out_shape=(shape, shape),
@@ -487,11 +485,12 @@
             dma((2, 2, FIELDS)), dma((2, 2, FIELDS)), dma((8,)), dma((8,)), dma((2, FIELDS, 8)), dma((2, FIELDS, 8)),
             wide, wide, field, field, wide, wide, field, field, field, field,
             floats(STEPS - 1, CELLS), floats(STEPS - 1, 3, CELLS), floats(16, 2 * NY), floats(16, 2 * NY),
-            floats(FIELDS, 16, 8, 8), floats(2, FIELDS, 8, 8, 8), floats(FIELDS, 4, TILES, 8, 8),
-            floats(2, FIELDS, 2, 8, 8), floats(2, FIELDS, TILES, 8, 8),
-            floats(FIELDS, 8, 4, 8), floats(FIELDS, 8, 4, 8),
-            dma((2, FIELDS, 8)), dma((2, FIELDS, 8)), dma((2, 2, FIELDS)), dma((2, 2, FIELDS)),
-            dma((FIELDS, 8)), dma((FIELDS, 8)), dma((2, 8)), dma((2, 8)),
+            floats(FIELDS, 16, 8, 8), floats(2, FIELDS, 8, 8, 8), floats(FIELDS, HALVES, 4, TILES, 4, 8),
+            floats(2, FIELDS, HALVES, 2, 4, 8), floats(2, FIELDS, HALVES, TILES, 4, 8),
+            floats(FIELDS, HALVES, 8, 2, 8), floats(FIELDS, HALVES, 8, 2, 8), floats(FIELDS, HALVES, 8, 2, 8),
+            dma((2, FIELDS, 8)), dma((2, FIELDS, 8)),
+            dma((2, 2, FIELDS, HALVES)), dma((2, 2, FIELDS, HALVES)),
+            dma((FIELDS, HALVES, 8)), dma((FIELDS, HALVES, 8)), dma((FIELDS, HALVES, 8)), dma((FIELDS, HALVES, 8)),
         ],
         compiler_params=pltpu.CompilerParams(
             collective_id=0, has_side_effects=True, vmem_limit_bytes=56 * 1024 * 1024
@@ -501,7 +500,8 @@
         speed.reshape(TILES, 8, 8, NZ), density.reshape(TILES, 8, 8, NZ),
         fwd_state.reshape(1, 4, CELLS, NZ), adj_state.reshape(1, 4, CELLS, NZ), *matrices,
     )
-    return tuple(grad.reshape(speed.shape) for grad in grads)
+    factor = 1.0 / math.sqrt(lax.axis_size("grp") * lax.axis_size("tile"))
+    return tuple(factor * grad.reshape(speed.shape) for grad in grads)
 
 
 def solution(mesh):

time: 72.9 us -> 70.8 us (0.971)
  local copies, waits for them, and re-layouts: 2.26 us -> 0 us
  Pallas kernels: 69.9 us -> 68.2 us
  other arithmetic: 0 us -> 1.69 us
    unnamed x4 -> x0, local copies, waits for them, and re-layouts: 2.26 us -> none
    pallas_call x1, Pallas kernels: 69.9 us -> 68.2 us  [per_device(): pl.pallas_call(kernel, out_shape=(shape, shape), in_specs=[smem] * 5 + [w...]
    mul x0 -> x1, other arithmetic: none -> 1.69 us  [per_device(): return tuple((factor * grad.reshape(speed.shape) for grad in grads))]
where the time goes in v3:
time: 70.8 us; the launch traced here: 70.5 us
  Pallas kernels  68.2 us (96%)
  other arithmetic  1.69 us (2%)
    pallas_call x1, Pallas kernels, per_device(): pl.pallas_call(kernel, out_shape=(shape, shape), in_specs=[smem] * 5 + [w...  68.2 us
    mul x1, other arithmetic, per_device(): return tuple((factor * grad.reshape(speed.shape) for grad in grads))  1.69 us

profile of v3, /device:TPU:2, one launch (start us, length us, event | category | flops | bytes accessed | tf_op | source)
XLA Modules:
  0.0 70.5 jit_solution(9175538046946236340)
XLA Ops:
  0.6 68.2 %shard_map.140 = (f32[4,8,8,128]{3,2,1,0:T(8,128)}, f32[4,8,8,128]{3,2,1,0:T(8,128)}) custom-call(s32[1,16]{1,0:T(1,128)} %ap.1, s32[1,3]{1,0:T(1,128)} %src.1, f32[1,4]{1,0:T(1,128)} %wave.1, s32[1,2,32]{2,1,0:T(2,128)} %bitcast.13, f32[1,4,32]{2,1,0:T(4,128)} %resid.1, f32[4,8,8,128]{3,2,1,0:T(8,128)} %bitcast.9, f32[4,8,8,128]{3,2,1,0:T(8,128)} %bitcast.10, ...), custom_call_target="tpu_custom_call" | custom-call | tf_op jit(solution)/shard_map/pallas_call | solution.py:475
  68.8 1.7 %broadcast_multiply_fusion = (f32[4,8,8,128]{3,2,1,0:T(8,128)}, f32[4,8,8,128]{3,2,1,0:T(8,128)}) fusion(f32[4,8,8,128]{3,2,1,0:T(8,128)} %get-tuple-element.5, f32[4,8,8,128]{3,2,1,0:T(8,128)} %get-tuple-element.4), kind=kLoop, calls=%fused_computation | loop fusion | flops 65536 | bytes 524288 | tf_op jit(solution)/shard_map/mul | solution.py:504

commit v4 on v3

--- a/solution.py
+++ b/solution.py
@@ -96,12 +96,12 @@
 
 def kernel(
     ap, src, wave, recs, resid, speed_in, density_in, fwd_in, adj_in, yplus_in, yminus_in, zplus_in, zminus_in,
-    grad_speed, grad_density,
+    bulk_sum, buoy_sum,
     speed, density, fwd, adj, yplus, yminus, zplus, zminus, in_sems,
     row, staged, bulk_tiles, buoy_tiles, codes, x_send, x_recv, c_send, c_recv, y_send, y_recv,
     pres, vel0, vel1, vel2, apres, avel0, avel1, avel2, bulk, buoy, dpres, dvel, bulk_image, buoy_image,
     image, came, part, passed, summed, total, terms, sums,
-    iy_send, iy_recv, ix_send, ix_recv, z_send, z_recv, g_send, g_recv,
+    iy_send, iy_recv, ix_send, ix_recv, z_send, z_recv, g_send, g_recv, keep_sems,
 ):
     z = lax.axis_index("grp")
     x, y, core = place()
@@ -119,17 +119,14 @@
             )
         )
     ]
-    for load in loads:
+    for load in loads[:2]:
         load.start()
     codes[0] = jnp.zeros((8, NZ), jnp.int32) + ap[0, 0]
     loads[0].wait()
-    loads[1].wait()
     for t in range(TILES):
-        dense = density[t]
-        row[1, x, t] = 1.0 / dense
-    for t in range(TILES):
-        dense, fast = density[t], speed[t]
-        row[0, x, t] = dense * fast * fast
+        row[1, x, t] = 1.0 / density[t]
+    for load in loads[2:]:
+        load.start()
     models, images = (bulk_tiles, buoy_tiles), (bulk_image, buoy_image)
     xl, xr, x2 = lax.rem(x + 3, 4), lax.rem(x + 1, 4), lax.rem(x + 2, 4)
     other, same = lax.rem(x + 1, 2), lax.rem(x, 2)
@@ -149,12 +146,16 @@
         return remote(part, part, x_send.at[1, side, f], x_recv.at[1, side, f], (right, left)[side])
 
     ready()
-    for f in (1, 0):
-        for side in range(2):
-            start(row_copy(f, side, x))
-        if f == 1:
-            for j in range(1, 8):
-                start(remote(codes.at[0], codes.at[j], c_send.at[j], c_recv.at[j], ahead[j]))
+    for side in range(2):
+        start(row_copy(1, side, x))
+    for j in range(1, 8):
+        start(remote(codes.at[0], codes.at[j], c_send.at[j], c_recv.at[j], ahead[j]))
+    loads[1].wait()
+    for t in range(TILES):
+        fast = speed[t]
+        row[0, x, t] = density[t] * fast * fast
+    for side in range(2):
+        start(row_copy(0, side, x))
 
     edge = jnp.zeros((PAD, NZ), jnp.float32)
     for ref in (pres, vel0, apres, avel0):
@@ -343,23 +344,25 @@
 
     lax.fori_loop(0, STEPS - 2, back_step, 0)
 
-    def image_copy(own, parity, f, j):
+    def image_copy(own, parity, f, h, j):
         target = lax.rem(y + j // 2, 4) * 2 + lax.rem(core + j % 2, 2)
+        rows = pl.ds(4 * h, 4)
         return remote(
-            image.at[f, parity * 8 + target], came.at[own, f, j], iy_send.at[own, f, j], iy_recv.at[own, f, j], ahead[j]
+            image.at[f, parity * 8 + target, rows], came.at[own, f, j, rows],
+            iy_send.at[own, f, h, j], iy_recv.at[own, f, h, j], ahead[j],
         )
 
     def send_image(f):
         for r in range(16):
             image[f, r] = images[f][(r + 16 - corner) & 15].reshape(8, 8, NZ)
         for own, parity in ((1, same), (0, other)):
-            for j in ORDER:
-                start(image_copy(own, parity, f, j))
+            for h in range(HALVES):
+                for j in ORDER:
+                    start(image_copy(own, parity, f, h, j))
 
     def collect(own, parity, f, h):
-        if h == 0:
-            for j in range(1, 8):
-                image_copy(own, parity, f, j).wait_recv()
+        for j in range(1, 8):
+            image_copy(own, parity, f, h, j).wait_recv()
         found = [matches(codes[j], parity * 8 + mine) for j in range(8)]
         rows = pl.ds(4 * h, 4)
         for high in range(2):
@@ -379,74 +382,80 @@
             origin, landing = part.at[f, h, target], summed.at[side, f, h]
         return remote(origin, landing, ix_send.at[stage, side, f, h], ix_recv.at[stage, side, f, h], device)
 
-    def collect_same(f):
-        for h in range(HALVES):
-            collect(1, same, f, h)
-            for side in range(2):
-                start(hop(0, side, f, h))
-
-    def collect_other(f):
-        for h in range(HALVES):
-            collect(0, other, f, h)
-            for side, target in ((0, xr), (1, xl)):
-                hop(0, side, f, h).wait_recv()
-                for i in range(2):
-                    part[f, h, target, 2 * side + i] += passed[side, f, h, i]
-                start(hop(1, side, f, h))
+    def collect_same(f, h):
+        collect(1, same, f, h)
+        for side in range(2):
+            start(hop(0, side, f, h))
+
+    def collect_other(f, h):
+        collect(0, other, f, h)
+        for side, target in ((0, xr), (1, xl)):
+            hop(0, side, f, h).wait_recv()
+            for i in range(2):
+                part[f, h, target, 2 * side + i] += passed[side, f, h, i]
+            start(hop(1, side, f, h))
 
     def piece_copy(f, h, d):
         return remote(
             total.at[f, h, lax.rem(z + d, 8)], terms.at[f, h, d], z_send.at[f, h, d], z_recv.at[f, h, d], column[d]
         )
 
+    outputs = (bulk_sum, buoy_sum)
+
+    def place_of(f, h, piece):
+        return outputs[f].at[piece // 2, pl.ds(4 * h + 2 * lax.rem(piece, 2), 2)]
+
     def result_copy(f, h, d, piece):
-        part_sum = sums.at[f, h, piece]
-        return remote(part_sum, part_sum, g_send.at[f, h, d], g_recv.at[f, h, d], column[d])
-
-    def send_pieces(f):
-        for h in range(HALVES):
-            for side in range(2):
-                hop(1, side, f, h).wait_recv()
-            for t in range(TILES):
-                whole = part[f, h, x, t] + summed[0, f, h, t] + summed[1, f, h, t]
-                total[f, h, 2 * t] = whole[:2]
-                total[f, h, 2 * t + 1] = whole[2:]
-            for d in FAR:
-                start(piece_copy(f, h, d))
-
-    def finish_pieces(f):
-        for h in range(HALVES):
-            held = total[f, h, z]
-            for d in range(1, 8):
-                piece_copy(f, h, d).wait_recv()
-                held = held + terms[f, h, d]
-            sums[f, h, z] = held
-            for d in FAR:
-                start(result_copy(f, h, d, z))
+        return remote(sums.at[f, h], place_of(f, h, piece), g_send.at[f, h, d], g_recv.at[f, h, d], column[d])
+
+    def keep_copy(f, h):
+        return pltpu.make_async_copy(sums.at[f, h], place_of(f, h, z), keep_sems.at[f, h])
+
+    def send_pieces(f, h):
+        for side in range(2):
+            hop(1, side, f, h).wait_recv()
+        for t in range(TILES):
+            whole = part[f, h, x, t] + summed[0, f, h, t] + summed[1, f, h, t]
+            total[f, h, 2 * t] = whole[:2]
+            total[f, h, 2 * t + 1] = whole[2:]
+        for d in FAR:
+            start(piece_copy(f, h, d))
+
+    def finish_pieces(f, h):
+        held = total[f, h, z]
+        for d in range(1, 8):
+            piece_copy(f, h, d).wait_recv()
+            held = held + terms[f, h, d]
+        sums[f, h] = held
+        keep_copy(f, h).start()
+        for d in FAR:
+            start(result_copy(f, h, d, z))
 
     adjoint_velocities(0)
     send_image(1)
     adjoint_pressure(0)
     send_image(0)
-    collect_same(1)
-    collect_other(1)
-    collect_same(0)
-    send_pieces(1)
-    collect_other(0)
-    send_pieces(0)
-    finish_pieces(1)
-    finish_pieces(0)
+    for h in range(HALVES):
+        collect_same(1, h)
+    for h in range(HALVES):
+        collect_other(1, h)
+    for h in range(HALVES):
+        collect_same(0, h)
+        send_pieces(1, h)
+    for h in range(HALVES):
+        collect_other(0, h)
+    for h in range(HALVES):
+        send_pieces(0, h)
+    for f in (1, 0):
+        for h in range(HALVES):
+            finish_pieces(f, h)
     for f in (1, 0):
         for h in range(HALVES):
             for d in range(1, 8):
                 result_copy(f, h, d, lax.rem(z + 8 - d, 8)).wait_recv()
-    for h in range(HALVES):
-        for piece in range(8):
-            t, spot = piece // 2, pl.ds(4 * h + 2 * (piece % 2), 2)
-            fast, dense = speed[t, spot], density[t, spot]
-            stiff, light = sums[0, h, piece], sums[1, h, piece]
-            grad_speed[t, spot] = stiff * (2.0 * dense * fast)
-            grad_density[t, spot] = stiff * (fast * fast) - light / (dense * dense)
+    for f in range(FIELDS):
+        for h in range(HALVES):
+            keep_copy(f, h).wait()
     for copy in pending:
         copy.wait_send()
 
@@ -459,7 +468,6 @@
         for m in (yplus, -yplus.T, np.concatenate([zplus.T, zplus.T]), np.concatenate([-zplus, -zplus]))
     ]
     smem = pl.BlockSpec(memory_space=pltpu.SMEM)
-    vmem = pl.BlockSpec(memory_space=pltpu.VMEM)
     whole = pl.BlockSpec(memory_space=pl.ANY)
     dma = pltpu.SemaphoreType.DMA
 
@@ -472,11 +480,11 @@
     tiles = floats(TILES, 8, 8)
     field, wide = floats(CELLS), floats(CELLS + 2 * PAD)
     shape = jax.ShapeDtypeStruct((TILES, 8, 8, NZ), jnp.float32)
-    grads = pl.pallas_call(
+    sums = pl.pallas_call(
         kernel,
         out_shape=(shape, shape),
         in_specs=[smem] * 5 + [whole] * 8,
-        out_specs=(vmem, vmem),
+        out_specs=(whole, whole),
         scratch_shapes=[
             tiles, tiles, halves(1, 4, CELLS, NZ), halves(1, 4, CELLS, NZ),
             halves(GROUP, GROUP), halves(GROUP, GROUP), halves(2 * NZ, NZ), halves(2 * NZ, NZ), dma((8,)),
@@ -487,10 +495,11 @@
             floats(STEPS - 1, CELLS), floats(STEPS - 1, 3, CELLS), floats(16, 2 * NY), floats(16, 2 * NY),
             floats(FIELDS, 16, 8, 8), floats(2, FIELDS, 8, 8, 8), floats(FIELDS, HALVES, 4, TILES, 4, 8),
             floats(2, FIELDS, HALVES, 2, 4, 8), floats(2, FIELDS, HALVES, TILES, 4, 8),
-            floats(FIELDS, HALVES, 8, 2, 8), floats(FIELDS, HALVES, 8, 2, 8), floats(FIELDS, HALVES, 8, 2, 8),
-            dma((2, FIELDS, 8)), dma((2, FIELDS, 8)),
+            floats(FIELDS, HALVES, 8, 2, 8), floats(FIELDS, HALVES, 8, 2, 8), floats(FIELDS, HALVES, 2, 8),
+            dma((2, FIELDS, HALVES, 8)), dma((2, FIELDS, HALVES, 8)),
             dma((2, 2, FIELDS, HALVES)), dma((2, 2, FIELDS, HALVES)),
             dma((FIELDS, HALVES, 8)), dma((FIELDS, HALVES, 8)), dma((FIELDS, HALVES, 8)), dma((FIELDS, HALVES, 8)),
+            dma((FIELDS, HALVES)),
         ],
         compiler_params=pltpu.CompilerParams(
             collective_id=0, has_side_effects=True, vmem_limit_bytes=56 * 1024 * 1024
@@ -500,8 +509,11 @@
         speed.reshape(TILES, 8, 8, NZ), density.reshape(TILES, 8, 8, NZ),
         fwd_state.reshape(1, 4, CELLS, NZ), adj_state.reshape(1, 4, CELLS, NZ), *matrices,
     )
+    bulk_sum, buoy_sum = (values.reshape(speed.shape) for values in sums)
     factor = 1.0 / math.sqrt(lax.axis_size("grp") * lax.axis_size("tile"))
-    return tuple(factor * grad.reshape(speed.shape) for grad in grads)
+    grad_speed = factor * (bulk_sum * (2.0 * density * speed))
+    grad_density = factor * (bulk_sum * (speed * speed) - buoy_sum / (density * density))
+    return grad_speed, grad_density
 
 
 def solution(mesh):

time: 70.8 us -> 69.5 us (0.982)
  Pallas kernels: 68.2 us -> 67 us
    pallas_call x1, Pallas kernels: 68.2 us -> 67 us  [per_device(): pl.pallas_call(kernel, out_shape=(shape, shape), in_specs=[smem] * 5 + [w...]
where the time goes in v4:
time: 69.5 us; the launch traced here: 69.4 us
  Pallas kernels  67 us (96%)
  other arithmetic  1.72 us (2%)
    pallas_call x1, Pallas kernels, per_device(): pl.pallas_call(kernel, out_shape=(shape, shape), in_specs=[smem] * 5 + [w...  67 us
    mul x1, other arithmetic, per_device(): factor * (bulk_sum * (speed * speed) - buoy_sum / (density * density))  1.72 us

profile of v4, /device:TPU:2, one launch (start us, length us, event | category | flops | bytes accessed | tf_op | source)
XLA Modules:
  0.0 69.4 jit_solution(8997237675928280673)
XLA Ops:
  0.6 0.0 copy-start
  0.6 0.0 copy-start.1
  0.7 67.0 %shard_map.140 = (f32[4,8,8,128]{3,2,1,0:T(8,128)}, f32[4,8,8,128]{3,2,1,0:T(8,128)}) custom-call(s32[1,16]{1,0:T(1,128)} %ap.1, s32[1,3]{1,0:T(1,128)} %src.1, f32[1,4]{1,0:T(1,128)} %wave.1, s32[1,2,32]{2,1,0:T(2,128)} %bitcast.26, f32[1,4,32]{2,1,0:T(4,128)} %resid.1, f32[4,8,8,128]{3,2,1,0:T(8,128)} %bitcast.23, f32[4,8,8,128]{3,2,1,0:T(8,128)} %bitcast.22, ...), custom_call_target="tpu_custom_call" | custom-call | tf_op jit(solution)/shard_map/pallas_call | solution.py:483
  67.6 0.0 copy-done
  67.6 0.0 copy-done.1
  67.6 1.7 %fusion.1 = (f32[4,2,32,128]{3,2,1,0:T(8,128)}, f32[4,2,32,128]{3,2,1,0:T(8,128)}) fusion(f32[4,2,32,128]{3,2,1,0:T(8,128)S(1)} %copy-done, f32[4,2,32,128]{3,2,1,0:T(8,128)S(1)} %copy-done.1, f32[4,2,32,128]{3,2,1,0:T(8,128)} %bitcast.25, f32[4,2,32,128]{3,2,1,0:T(8,128)} %bitcast.24), kind=kLoop, calls=%fused_computation.2 | loop fusion | flops 327680 | bytes 786432 | tf_op jit(solution)/shard_map/mul | solution.py:515
Async XLA Ops:
  0.6 67.0 %copy-start = (f32[4,2,32,128]{3,2,1,0:T(8,128)S(1)}, f32[4,2,32,128]{3,2,1,0:T(8,128)}, u32[]{:S(2)}) copy-start(f32[4,2,32,128]{3,2,1,0:T(8,128)} %param.14) | copy-start | bytes 393220
  0.6 67.0 %copy-start.1 = (f32[4,2,32,128]{3,2,1,0:T(8,128)S(1)}, f32[4,2,32,128]{3,2,1,0:T(8,128)}, u32[]{:S(2)}) copy-start(f32[4,2,32,128]{3,2,1,0:T(8,128)} %param.13) | copy-start | bytes 393220

commit v5 on v4

--- a/solution.py
+++ b/solution.py
@@ -90,7 +90,7 @@
     ]
 
 
-ORDER = (4, 5, 2, 3, 6, 7, 1)
+ORDER = (2, 6, 4, 3, 7, 5, 1)
 FAR = (4, 3, 5, 2, 6, 1, 7)
 
 

time: 69.5 us -> 69.3 us (level)
  no operation moved by 1% of the time
where the time goes in v5:
time: 69.3 us; the launch traced here: 69 us
  Pallas kernels  66.6 us (96%)
  other arithmetic  1.72 us (2%)
    pallas_call x1, Pallas kernels, per_device(): pl.pallas_call(kernel, out_shape=(shape, shape), in_specs=[smem] * 5 + [w...  66.6 us
    mul x1, other arithmetic, per_device(): factor * (bulk_sum * (speed * speed) - buoy_sum / (density * density))  1.72 us

profile of v5, /device:TPU:2, one launch (start us, length us, event | category | flops | bytes accessed | tf_op | source)
XLA Modules:
  0.0 69.0 jit_solution(4482579096217486816)
XLA Ops:
  0.6 0.0 copy-start
  0.6 0.0 copy-start.1
  0.7 66.6 %shard_map.140 = (f32[4,8,8,128]{3,2,1,0:T(8,128)}, f32[4,8,8,128]{3,2,1,0:T(8,128)}) custom-call(s32[1,16]{1,0:T(1,128)} %ap.1, s32[1,3]{1,0:T(1,128)} %src.1, f32[1,4]{1,0:T(1,128)} %wave.1, s32[1,2,32]{2,1,0:T(2,128)} %bitcast.26, f32[1,4,32]{2,1,0:T(4,128)} %resid.1, f32[4,8,8,128]{3,2,1,0:T(8,128)} %bitcast.23, f32[4,8,8,128]{3,2,1,0:T(8,128)} %bitcast.22, ...), custom_call_target="tpu_custom_call" | custom-call | tf_op jit(solution)/shard_map/pallas_call | solution.py:483
  67.3 0.0 copy-done
  67.3 0.0 copy-done.1
  67.3 1.7 %fusion.1 = (f32[4,2,32,128]{3,2,1,0:T(8,128)}, f32[4,2,32,128]{3,2,1,0:T(8,128)}) fusion(f32[4,2,32,128]{3,2,1,0:T(8,128)S(1)} %copy-done, f32[4,2,32,128]{3,2,1,0:T(8,128)S(1)} %copy-done.1, f32[4,2,32,128]{3,2,1,0:T(8,128)} %bitcast.25, f32[4,2,32,128]{3,2,1,0:T(8,128)} %bitcast.24), kind=kLoop, calls=%fused_computation.2 | loop fusion | flops 327680 | bytes 786432 | tf_op jit(solution)/shard_map/mul | solution.py:515
Async XLA Ops:
  0.6 66.7 %copy-start = (f32[4,2,32,128]{3,2,1,0:T(8,128)S(1)}, f32[4,2,32,128]{3,2,1,0:T(8,128)}, u32[]{:S(2)}) copy-start(f32[4,2,32,128]{3,2,1,0:T(8,128)} %param.14) | copy-start | bytes 393220
  0.6 66.7 %copy-start.1 = (f32[4,2,32,128]{3,2,1,0:T(8,128)S(1)}, f32[4,2,32,128]{3,2,1,0:T(8,128)}, u32[]{:S(2)}) copy-start(f32[4,2,32,128]{3,2,1,0:T(8,128)} %param.13) | copy-start | bytes 393220
